TPU v7x, 256 devices: a whole 4x4x8 slice. The times are simulated.
256 devices in a mesh: gx: 16 (over x, y), gz: 8 (over z), gy: 2 (over core).
Axes of the slice: x: 4, y: 4, z: 8, core: 2. Of those that a mesh axis runs over, the one named last changes fastest.
Arguments:
- blocks: bfloat16 [16, 8, 4, 96, 4096], P('gx', 'gz', 'gy'), may hold values from -6 to 6
- block_count: int32 [16, 8, 2], P('gx', 'gz', 'gy'), may hold values from 1 to 2, as said below
- neighbours: int32 [16, 8, 4, 26], P('gx', 'gz', 'gy'), may hold values from -1 to 15, as said below
- conv_weight: bfloat16 [48, 2592], replicated, may hold values from -0.125 to 0.125
- conv_bias: float32 [48], replicated, may hold values from -3 to 3
- head_weight: bfloat16 [48, 48], replicated, may hold values from -0.875 to 0.875
- head_bias: float32 [48], replicated, may hold values from -3 to 3
Outputs:
- features: bfloat16 [16, 8, 4, 48, 4096], P('gx', 'gz', 'gy')
Inputs may be any that keep to these rules, and one draw needn't show every extreme that they name: Each device's foreground blocks fill its first block_count slots; some device fills all 2. `neighbours`: -1 means no foreground block at that offset. Otherwise the value is u + 2 c: used slot u of the device reached from this one by the offset's steps along the axes whose bits are set in c (bit 0 x, bit 1 y, bit 2 z); bits are set only on axes where the offset is nonzero, and c = 0 names this device. Unused slots hold -1 everywhere. Each device's blocks sit at distinct positions of its own region of 2 x 2 x 4 block positions, and the links follow that geometry. The most is reached in every draw.
All inputs are finite; a program needn't handle non-finite values.
Results may differ from a plain program's by a relative error of at most 0.0046.
Values may be sent and summed in bfloat16 or wider, within the bound.
No kernel may reach another device: no remote copies, remote signals or barrier semaphores. Data moves between devices by JAX's collectives and lax.ppermute only.
A program may use at most 128 MiB of HBM per device.

v0:
```python
import math

import jax
import jax.numpy as jnp
from jax import lax
from jax.sharding import PartitionSpec as P

COUT = 48
EDGE = 16
VOX = 4096


def from_behind(value, axis, by):
    length = lax.axis_size(axis)
    pairs = [(i, i + by) for i in range(length) if 0 <= i + by < length]
    return lax.ppermute(value, axis, pairs)


def offset_list():
    return [
        (step_x, step_y, step_z)
        for step_x in (-1, 0, 1)
        for step_y in (-1, 0, 1)
        for step_z in (-1, 0, 1)
    ]


def edge_piece(volume, offsets, first_axis):
    piece = volume
    for axis_id in range(3):
        dim = first_axis + axis_id
        length = piece.shape[dim]
        if offsets[axis_id] == -1:
            piece = lax.slice_in_dim(piece, length - 1, length, axis=dim)
        elif offsets[axis_id] == 1:
            piece = lax.slice_in_dim(piece, 0, 1, axis=dim)
    return piece


def assemble(pieces, first_axis):
    layers_x = []
    for step_x in (-1, 0, 1):
        layers_y = []
        for step_y in (-1, 0, 1):
            layers_y.append(
                jnp.concatenate(
                    [pieces[step_x, step_y, step_z] for step_z in (-1, 0, 1)], first_axis + 2
                )
            )
        layers_x.append(jnp.concatenate(layers_y, first_axis + 1))
    return jnp.concatenate(layers_x, first_axis)


def convolve_padded(padded, conv_weight, conv_bias, head_weight, head_bias):
    channels = padded.shape[0]
    edge = padded.shape[1] - 2
    total = jnp.zeros((conv_weight.shape[0], edge * edge * edge), jnp.float32)
    for tap, offsets in enumerate(offset_list()):
        view = padded[
            :,
            1 + offsets[0] : 1 + offsets[0] + edge,
            1 + offsets[1] : 1 + offsets[1] + edge,
            1 + offsets[2] : 1 + offsets[2] + edge,
        ]
        total = total + jnp.dot(
            conv_weight[:, tap * channels : (tap + 1) * channels],
            view.reshape(channels, -1),
            preferred_element_type=jnp.float32,
        )
    hidden = jnp.maximum(total + conv_bias[:, None], 0.0).astype(jnp.bfloat16)
    mixed = jnp.dot(head_weight, hidden, preferred_element_type=jnp.float32) + head_bias[:, None]
    return mixed.astype(jnp.bfloat16)


def pack_pieces(pieces):
    return jnp.concatenate([piece.reshape(piece.shape[0], -1) for piece in pieces], 1)


def unpack_pieces(joined, pieces):
    results = []
    start = 0
    for piece in pieces:
        width = math.prod(piece.shape[1:])
        results.append(joined[:, start : start + width].reshape(piece.shape))
        start += width
    return results


def along_x(pieces, offset):
    moved = from_behind(pack_pieces(pieces), "gx", offset)
    return unpack_pieces(moved, pieces)


def along_y(pieces, offset):
    moved = from_behind(pack_pieces(pieces), "gy", offset)
    return unpack_pieces(moved, pieces)


def along_z(pieces, offset):
    moved = from_behind(pack_pieces(pieces), "gz", offset)
    return unpack_pieces(moved, pieces)


def body(blocks, block_count, neighbours, conv_weight, conv_bias, head_weight, head_bias):
    slot_total = blocks.shape[2]
    channels = blocks.shape[3]
    volumes = blocks.reshape(slot_total, channels, EDGE, EDGE, EDGE)
    filled = block_count.reshape(())
    face_links = neighbours.reshape(slot_total, 26)
    received = {(0, 0, 0): volumes}
    for axis_id, mover in ((0, along_x), (1, along_y), (2, along_z)):
        sources = list(received.items())
        for sense in (-1, 1):
            direction = [0, 0, 0]
            direction[axis_id] = sense
            outgoing = [
                edge_piece(source_value, tuple(direction), 2)
                for source_key, source_value in sources
            ]
            arrived = mover(outgoing, 1 if sense == -1 else -1)
            for (source_key, source_value), landed in zip(sources, arrived):
                new_key = list(source_key)
                new_key[axis_id] = sense
                received[tuple(new_key)] = landed
    pieces = {(0, 0, 0): volumes}
    link_index = 0
    for offsets in offset_list():
        if offsets == (0, 0, 0):
            continue
        candidates = []
        codes = []
        for code in range(8):
            if any((code >> axis_id & 1 and offsets[axis_id] == 0 for axis_id in range(3))):
                continue
            source_key = tuple(
                (offsets[axis_id] if code >> axis_id & 1 else 0 for axis_id in range(3))
            )
            remaining = tuple(
                (0 if code >> axis_id & 1 else offsets[axis_id] for axis_id in range(3))
            )
            candidates.append(edge_piece(received[source_key], remaining, 2))
            codes.append(code)
        pool = jnp.concatenate(candidates, 0)
        link = face_links[:, link_index]
        link_index += 1
        clean = jnp.maximum(link, 0)
        code_now = clean // slot_total
        rank = jnp.zeros_like(clean)
        for known in codes:
            rank = rank + (code_now > known).astype(jnp.int32)
        chosen = jnp.take(pool, rank * slot_total + clean % slot_total, axis=0)
        pieces[offsets] = jnp.where(
            (link >= 0)[:, None, None, None, None], chosen, jnp.zeros_like(chosen)
        )
    padded_all = assemble(pieces, 2)

    def compute_slot(slot_id, outputs):
        padded = lax.dynamic_index_in_dim(padded_all, slot_id, 0, keepdims=False)
        result = convolve_padded(padded, conv_weight, conv_bias, head_weight, head_bias)
        return lax.dynamic_update_index_in_dim(outputs, result, slot_id, 0)

    empty = jnp.zeros((slot_total, COUT, VOX), jnp.bfloat16)
    outputs = lax.fori_loop(0, filled, compute_slot, empty)
    return outputs.reshape(1, 1, slot_total, COUT, VOX)


def solution(mesh):
    placed = (
        P("gx", "gz", "gy", None, None),
        P("gx", "gz", "gy"),
        P("gx", "gz", "gy", None),
        P(),
        P(),
        P(),
        P(),
    )
    return jax.shard_map(
        body, mesh=mesh, in_specs=placed, out_specs=P("gx", "gz", "gy", None, None), check_vma=False
    )
```

profile of v0, /device:TPU:103, one launch (start us, length us, event | category | flops | bytes accessed | tf_op | source)
XLA Modules:
  0.0 389.8 jit_solution(18363705515192925839)
XLA Ops:
  0.0 5.2 %copy.165 = bf16[1,1,2,96,4096]{3,2,4,1,0:T(2,128)(2,1)S(1)} copy(bf16[1,1,2,96,4096]{4,3,2,1,0:T(8,128)(2,1)} %param.23) | data formatting | bytes 3145728 | tf_op args[0]
  6.0 1.5 reshape.834
  7.5 3.2 collective-permute-start
  11.3 1.5 reshape.838
  12.8 4.6 %collective-permute-start.1 = (bf16[2,24576]{1,0:T(2,128)(2,1)}, bf16[2,24576]{1,0:T(2,128)(2,1)}, u32[]{:S(2)}, u32[]{:S(2)}) collective-permute-start(bf16[2,24576]{1,0:T(2,128)(2,1)} %reshape.838), channel_id=1, source_target_pairs={{16,0},{32,16},{48,32},{64,48},{80,64},{96,80},{112,96},{128,112},... | collective-permute-start | bytes 294920 | tf_op jit(solution)/shard_map/ppermute | solution.py:16
  50.3 1.6 copy.184
  64.8 1.9 maximum_bitcast_fusion
  76.4 13.1 %pad_maximum_fusion = bf16[2,27648]{1,0:T(2,128)(2,1)} fusion(bf16[2,1536]{1,0:T(2,128)(2,1)S(1)} %reshape.840, bf16[2,1536]{1,0:T(2,128)(2,1)S(1)} %reshape.837, bf16[2,24576]{1,0:T(2,128)(2,1)} %reshape.836), kind=kLoop, calls=%fused_computation.121 | loop fusion | flops 331776 | bytes 221184 | tf_op jit(solution)/shard_map/concatenate | solution.py:76
  92.2 1.6 broadcast_select_fusion.11
  93.7 1.5 broadcast_select_fusion.6
  95.2 1.7 pad_maximum_fusion.1
  102.9 4.4 %collective-permute-start.3 = (bf16[2,27648]{1,0:T(2,128)(2,1)}, bf16[2,27648]{1,0:T(2,128)(2,1)}, u32[]{:S(2)}, u32[]{:S(2)}) collective-permute-start(bf16[2,27648]{1,0:T(2,128)(2,1)} %pad_maximum_fusion.1), channel_id=1, source_target_pairs={{1,0},{3,2},{5,4},{7,6},{9,8},{11,10},{13,12},{15,14},{17,16},{19,... | collective-permute-start | bytes 331784 | tf_op jit(solution)/shard_map/ppermute | solution.py:16
  111.4 1.6 slice.975
  115.7 1.6 maximum_bitcast_fusion.1
  128.1 1.8 concatenate.131
  129.9 4.7 %collective-permute-start.4 = (bf16[2,31104]{1,0:T(2,128)(2,1)}, bf16[2,31104]{1,0:T(2,128)(2,1)}, u32[]{:S(2)}, u32[]{:S(2)}) collective-permute-start(bf16[2,31104]{1,0:T(2,128)(2,1)} %concatenate.131), channel_id=1, source_target_pairs={{0,2},{2,4},{4,6},{6,8},{8,10},{10,12},{12,14},{1,3},{3,5},{5,7},{... | collective-permute-start | bytes 373256 | tf_op jit(solution)/shard_map/ppermute | solution.py:16
  134.6 1.8 concatenate.134
  136.4 1.9 collective-permute-start.5
  145.3 1.5 broadcast_select_fusion.7
  213.5 56.4 %maximum_maximum_fusion = bf16[2,96,18,18,18]{1,0,4,3,2:T(2,128)(2,1)S(1)} fusion(bf16[2,96,1,1,1]{1,0,4,3,2:T(2,128)(2,1)S(1)} %broadcast_select_fusion.44, bf16[2,96,1,1,16]{1,0,4,3,2:T(2,128)(2,1)} %get-tuple-element.416, bf16[2,96,1,1,1]{1,0,4,3,2:T(2,128)(2,1)S(1)} %broadcast_select_fusion.45, bf16[2,96,1,16,1]{1,0,4,3,2:T(2,128)(2,1)S(1)} %get-tuple-element.418, ...), kind=kLoop, calls=%fused_computation.102 | loop fusion | flops 29113344 | bytes 4478976 | tf_op jit(solution)/shard_map/concatenate | solution.py:51
  270.0 2.4 copy.310
  273.3 116.2 %while.10 = (s32[]{:T(128)}, bf16[2,48,4096]{2,1,0:T(8,128)(2,1)}, s32[]{:T(128)}, bf16[2,96,18,18,18]{1,4,3,2,0:T(8,128)(2,1)}, bf16[48,2592]{1,0:T(8,128)(2,1)...) while((s32[]{:T(128)}, bf16[2,48,4096]{2,1,0:T(8,128)(2,1)}, ...), condition=%wide.region_1.9_spmd, body=%wide.region_0.8_spmd.sunk | while | flops 1044185088 | bytes 148722096 | solution.py:163
  274.2 1.9 dynamic-slice_bitcast_fusion.2
  276.1 2.1 fusion.385
  286.9 2.1 convolution_add_fusion.38
  289.0 7.7 %fusion.384 = (bf16[96,16,16,16]{0,3,2,1:T(8,128)(2,1)S(1)}, bf16[96,16,16,16]{0,3,2,1:T(8,128)(2,1)}, bf16[96,16,16,16]{0,3,2,1:T(8,128)(2,1)}, bf16[96,16,16,1...) fusion(bf16[96,18,18,18]{0,3,2,1:T(8,128)(2,1)S(1)} %dynamic-sl, ...), kind=kLoop, calls=%fused_computation.725.clone.1 | loop fusion | bytes 29884416 | tf_op jit(solution)/shard_map/while/body/slice | solution.py:59
  296.7 2.1 convolution_add_fusion.39
  308.2 2.2 fusion.387
  314.2 2.1 convolution_bitcast_fusion.22
  316.4 2.1 convolution_bitcast_fusion.23
  318.5 2.1 convolution_bitcast_fusion.24
  320.6 2.1 convolution_bitcast_fusion.25
  322.7 2.1 convolution_bitcast_fusion.26
  324.8 2.2 convolution_bitcast_fusion.27
  327.0 4.2 %fusion.388 = bf16[2,48,4096]{2,1,0:T(8,128)(2,1)} fusion(bf16[2,48,4096]{2,1,0:T(8,128)(2,1)} %get-tuple-element.574, s32[]{:T(128)S(6)} %select_n.973, bf16[48,48]{1,0:T(8,128)(2,1)S(1)} %get-tuple-element.590, f32[48,4096]{1,0:T(8,128)S(1)} %convolution_bitcast_fusion.19, f32[48,4096]{1,0:T(8,128)S(1)} %convolution_bitcast_fusion.20, ...), kind=kOutput, calls=%fused_computation.69.clone.1 | convolution fusion | flops 59572224 | bytes 9061252 | tf_op jit(solution)/shard_map/while/body/dot_general | solution.py:71
  331.9 1.9 dynamic-slice_bitcast_fusion.2
  333.8 2.1 fusion.385
  344.5 2.1 convolution_add_fusion.38
  346.7 7.7 %fusion.384 = (bf16[96,16,16,16]{0,3,2,1:T(8,128)(2,1)S(1)}, bf16[96,16,16,16]{0,3,2,1:T(8,128)(2,1)}, bf16[96,16,16,16]{0,3,2,1:T(8,128)(2,1)}, bf16[96,16,16,1...) fusion(bf16[96,18,18,18]{0,3,2,1:T(8,128)(2,1)S(1)} %dynamic-sl, ...), kind=kLoop, calls=%fused_computation.725.clone.1 | loop fusion | bytes 29884416 | tf_op jit(solution)/shard_map/while/body/slice | solution.py:59
  354.4 2.1 convolution_add_fusion.39
  365.9 2.2 fusion.387
  371.9 2.1 convolution_bitcast_fusion.22
  374.1 2.1 convolution_bitcast_fusion.23
  376.2 2.1 convolution_bitcast_fusion.24
  378.3 2.1 convolution_bitcast_fusion.25
  380.4 2.1 convolution_bitcast_fusion.26
  382.5 2.2 convolution_bitcast_fusion.27
  384.7 4.2 %fusion.388 = bf16[2,48,4096]{2,1,0:T(8,128)(2,1)} fusion(bf16[2,48,4096]{2,1,0:T(8,128)(2,1)} %get-tuple-element.574, s32[]{:T(128)S(6)} %select_n.973, bf16[48,48]{1,0:T(8,128)(2,1)S(1)} %get-tuple-element.590, f32[48,4096]{1,0:T(8,128)S(1)} %convolution_bitcast_fusion.19, f32[48,4096]{1,0:T(8,128)S(1)} %convolution_bitcast_fusion.20, ...), kind=kOutput, calls=%fused_computation.69.clone.1 | convolution fusion | flops 59572224 | bytes 9061252 | tf_op jit(solution)/shard_map/while/body/dot_general | solution.py:71
  (368 shorter events, 200.6 us)
Async XLA Ops:
  0.0 17.3 %copy-start.13 = (s32[1,1,2,26]{3,2,1,0:T(2,128)S(1)}, s32[1,1,2,26]{3,2,1,0:T(2,128)}, u32[]{:S(2)}) copy-start(s32[1,1,2,26]{3,2,1,0:T(2,128)} %param.25) | copy-start | bytes 628
  7.5 50.6 %collective-permute-start = (bf16[2,24576]{1,0:T(2,128)(2,1)}, bf16[2,24576]{1,0:T(2,128)(2,1)}, u32[]{:S(2)}, u32[]{:S(2)}) collective-permute-start(bf16[2,24576]{1,0:T(2,128)(2,1)} %reshape.834), channel_id=1, source_target_pairs={{0,16},{16,32},{32,48},{48,64},{64,80},{80,96},{96,112},{112,128},... | collective-permute-start | bytes 294920 | tf_op jit(solution)/shard_map/ppermute | solution.py:16
  12.8 54.0 %collective-permute-start.1 = (bf16[2,24576]{1,0:T(2,128)(2,1)}, bf16[2,24576]{1,0:T(2,128)(2,1)}, u32[]{:S(2)}, u32[]{:S(2)}) collective-permute-start(bf16[2,24576]{1,0:T(2,128)(2,1)} %reshape.838), channel_id=1, source_target_pairs={{16,0},{32,16},{48,32},{64,48},{80,64},{96,80},{112,96},{128,112},... | collective-permute-start | bytes 294920 | tf_op jit(solution)/shard_map/ppermute | solution.py:16
  89.4 17.8 %collective-permute-start.2 = (bf16[2,27648]{1,0:T(2,128)(2,1)}, bf16[2,27648]{1,0:T(2,128)(2,1)}, u32[]{:S(2)}, u32[]{:S(2)}) collective-permute-start(bf16[2,27648]{1,0:T(2,128)(2,1)} %pad_maximum_fusion), channel_id=1, source_target_pairs={{0,1},{2,3},{4,5},{6,7},{8,9},{10,11},{12,13},{14,15},{16,17},{18,... | collective-permute-start | bytes 331784 | tf_op jit(solution)/shard_map/ppermute | solution.py:16
  92.1 23.6 %copy-start.14 = (bf16[2,96,16,1,16]{1,0,4,3,2:T(2,128)(2,1)S(1)}, bf16[2,96,16,1,16]{1,0,4,3,2:T(2,128)(2,1)}, u32[]{:S(2)}) copy-start(bf16[2,96,16,1,16]{1,0,4,3,2:T(2,128)(2,1)} %get-tuple-element.294) | copy-start | bytes 294916
  102.9 8.5 %collective-permute-start.3 = (bf16[2,27648]{1,0:T(2,128)(2,1)}, bf16[2,27648]{1,0:T(2,128)(2,1)}, u32[]{:S(2)}, u32[]{:S(2)}) collective-permute-start(bf16[2,27648]{1,0:T(2,128)(2,1)} %pad_maximum_fusion.1), channel_id=1, source_target_pairs={{1,0},{3,2},{5,4},{7,6},{9,8},{11,10},{13,12},{15,14},{17,16},{19,... | collective-permute-start | bytes 331784 | tf_op jit(solution)/shard_map/ppermute | solution.py:16
  109.5 3.5 copy-start.15
  122.9 19.6 %copy-start.26 = (pred[2]{0:T(512)(128)(4,1)S(1)}, pred[2]{0:T(512)(128)(4,1)}, u32[]{:S(2)}) copy-start(pred[2]{0:T(512)(128)(4,1)} %get-tuple-element.162) | copy-start | bytes 10
  122.9 19.6 %copy-start.27 = (pred[2]{0:T(512)(128)(4,1)S(1)}, pred[2]{0:T(512)(128)(4,1)}, u32[]{:S(2)}) copy-start(pred[2]{0:T(512)(128)(4,1)} %get-tuple-element.456) | copy-start | bytes 10
  123.0 20.2 %copy-start.23 = (pred[2]{0:T(512)(128)(4,1)S(1)}, pred[2]{0:T(512)(128)(4,1)}, u32[]{:S(2)}) copy-start(pred[2]{0:T(512)(128)(4,1)} %get-tuple-element.167) | copy-start | bytes 10
  126.1 20.7 %copy-start.24 = (pred[2]{0:T(512)(128)(4,1)S(1)}, pred[2]{0:T(512)(128)(4,1)}, u32[]{:S(2)}) copy-start(pred[2]{0:T(512)(128)(4,1)} %get-tuple-element.138) | copy-start | bytes 10
  126.1 20.7 %copy-start.25 = (pred[2]{0:T(512)(128)(4,1)S(1)}, pred[2]{0:T(512)(128)(4,1)}, u32[]{:S(2)}) copy-start(pred[2]{0:T(512)(128)(4,1)} %get-tuple-element.144) | copy-start | bytes 10
  129.9 18.9 %collective-permute-start.4 = (bf16[2,31104]{1,0:T(2,128)(2,1)}, bf16[2,31104]{1,0:T(2,128)(2,1)}, u32[]{:S(2)}, u32[]{:S(2)}) collective-permute-start(bf16[2,31104]{1,0:T(2,128)(2,1)} %concatenate.131), channel_id=1, source_target_pairs={{0,2},{2,4},{4,6},{6,8},{8,10},{10,12},{12,14},{1,3},{3,5},{5,7},{... | collective-permute-start | bytes 373256 | tf_op jit(solution)/shard_map/ppermute | solution.py:16
  136.4 16.3 %collective-permute-start.5 = (bf16[2,31104]{1,0:T(2,128)(2,1)}, bf16[2,31104]{1,0:T(2,128)(2,1)}, u32[]{:S(2)}, u32[]{:S(2)}) collective-permute-start(bf16[2,31104]{1,0:T(2,128)(2,1)} %concatenate.134), channel_id=1, source_target_pairs={{2,0},{4,2},{6,4},{8,6},{10,8},{12,10},{14,12},{3,1},{5,3},{7,5},{... | collective-permute-start | bytes 373256 | tf_op jit(solution)/shard_map/ppermute | solution.py:16
  167.3 43.8 %copy-start.22 = (pred[2]{0:T(512)(128)(4,1)S(1)}, pred[2]{0:T(512)(128)(4,1)}, u32[]{:S(2)}) copy-start(pred[2]{0:T(512)(128)(4,1)} %get-tuple-element.164) | copy-start | bytes 10
  167.4 46.1 %copy-start.16 = (bf16[2,96,1,16,16]{1,0,4,3,2:T(2,128)(2,1)S(1)}, bf16[2,96,1,16,16]{1,0,4,3,2:T(2,128)(2,1)}, u32[]{:S(2)}) copy-start(bf16[2,96,1,16,16]{1,0,4,3,2:T(2,128)(2,1)} %broadcast_select_fusion.11) | copy-start | bytes 294916
  167.4 46.1 %copy-start.17 = (bf16[2,96,1,16,16]{1,0,4,3,2:T(2,128)(2,1)S(1)}, bf16[2,96,1,16,16]{1,0,4,3,2:T(2,128)(2,1)}, u32[]{:S(2)}) copy-start(bf16[2,96,1,16,16]{1,0,4,3,2:T(2,128)(2,1)} %broadcast_select_fusion.6) | copy-start | bytes 294916
  167.4 46.1 %copy-start.18 = (bf16[2,96,16,1,16]{1,0,4,3,2:T(2,128)(2,1)S(1)}, bf16[2,96,16,1,16]{1,0,4,3,2:T(2,128)(2,1)}, u32[]{:S(2)}) copy-start(bf16[2,96,16,1,16]{1,0,4,3,2:T(2,128)(2,1)} %broadcast_select_fusion.7) | copy-start | bytes 294916
  181.5 20.5 %copy-start.28 = (bf16[2,96]{1,0:T(2,128)(2,1)S(1)}, bf16[2,96]{1,0:T(2,128)(2,1)}, u32[]{:S(2)}) copy-start(bf16[2,96]{1,0:T(2,128)(2,1)} %gather_fusion.6) | copy-start | bytes 1156
  269.9 3.4 copy-start.19
  269.9 3.4 copy-start.20
  270.0 3.4 copy-start.21
  296.7 2.1 copy-start.12
  296.7 3.5 copy-start.11
  298.8 2.7 copy-start.10
  300.1 2.7 copy-start.9
  301.5 2.6 copy-start.8
  302.8 2.6 copy-start.7
  304.1 2.7 copy-start.6
  305.5 2.7 copy-start.5
  306.8 3.6 copy-start.4
  306.8 4.9 %copy-start.3 = (bf16[96,16,16,16]{0,3,2,1:T(8,128)(2,1)S(1)}, bf16[96,16,16,16]{0,3,2,1:T(8,128)(2,1)}, u32[]{:S(2)}) copy-start(bf16[96,16,16,16]{0,3,2,1:T(8,128)(2,1)} %get-tuple-element.536) | copy-start | bytes 2359300 | tf_op jit(solution)/shard_map/while
  308.2 4.8 %copy-start.2 = (bf16[96,16,16,16]{0,3,2,1:T(8,128)(2,1)S(1)}, bf16[96,16,16,16]{0,3,2,1:T(8,128)(2,1)}, u32[]{:S(2)}) copy-start(bf16[96,16,16,16]{0,3,2,1:T(8,128)(2,1)} %get-tuple-element.537) | copy-start | bytes 2359300 | tf_op jit(solution)/shard_map/while
  310.4 3.8 copy-start.1
  311.7 4.7 %copy-start = (bf16[96,16,16,16]{0,3,2,1:T(8,128)(2,1)S(1)}, bf16[96,16,16,16]{0,3,2,1:T(8,128)(2,1)}, u32[]{:S(2)}) copy-start(bf16[96,16,16,16]{0,3,2,1:T(8,128)(2,1)} %get-tuple-element.539) | copy-start | bytes 2359300 | tf_op jit(solution)/shard_map/while
  354.3 2.1 copy-start.12
  354.4 3.5 copy-start.11
  356.5 2.7 copy-start.10
  357.8 2.7 copy-start.9
  359.2 2.6 copy-start.8
  360.5 2.6 copy-start.7
  361.8 2.7 copy-start.6
  363.1 2.7 copy-start.5
  364.5 3.6 copy-start.4
  364.5 4.9 %copy-start.3 = (bf16[96,16,16,16]{0,3,2,1:T(8,128)(2,1)S(1)}, bf16[96,16,16,16]{0,3,2,1:T(8,128)(2,1)}, u32[]{:S(2)}) copy-start(bf16[96,16,16,16]{0,3,2,1:T(8,128)(2,1)} %get-tuple-element.536) | copy-start | bytes 2359300 | tf_op jit(solution)/shard_map/while
  365.9 4.8 %copy-start.2 = (bf16[96,16,16,16]{0,3,2,1:T(8,128)(2,1)S(1)}, bf16[96,16,16,16]{0,3,2,1:T(8,128)(2,1)}, u32[]{:S(2)}) copy-start(bf16[96,16,16,16]{0,3,2,1:T(8,128)(2,1)} %get-tuple-element.537) | copy-start | bytes 2359300 | tf_op jit(solution)/shard_map/while
  368.1 3.8 copy-start.1
  369.4 4.7 %copy-start = (bf16[96,16,16,16]{0,3,2,1:T(8,128)(2,1)S(1)}, bf16[96,16,16,16]{0,3,2,1:T(8,128)(2,1)}, u32[]{:S(2)}) copy-start(bf16[96,16,16,16]{0,3,2,1:T(8,128)(2,1)} %get-tuple-element.539) | copy-start | bytes 2359300 | tf_op jit(solution)/shard_map/while
where the time goes:
time: 398 us; the launch traced here: 390 us
  local copies, waits for them, and re-layouts  145 us (36%)
  other arithmetic  131 us (33%)
  matrix products  89.9 us (23%)
  starting transfers between devices  20.1 us (5%)
    dot_general x52, matrix products, convolve_padded(): jnp.dot(conv_weight[:, tap * channels:(tap + 1) * channels], view.reshape...  81.6 us
    concatenate x1, other arithmetic, assemble(): return jnp.concatenate(layers_x, first_axis)  56.4 us
    slice x43, local copies, waits for them, and re-layouts, edge_piece(): piece = lax.slice_in_dim(piece, length - 1, length, axis=dim)  26.7 us
    gather x26, local copies, waits for them, and re-layouts, body(): chosen = jnp.take(pool, rank * slot_total + clean % slot_total, axis=0)  23.3 us
    select_n x23, other arithmetic, body(): jnp.where((link >= 0)[:, None, None, None, None], chosen, jnp.zeros_like(...  20.9 us
    ppermute x6, starting transfers between devices, from_behind(): return lax.ppermute(value, axis, pairs)  20.1 us
    slice x4, local copies, waits for them, and re-layouts, convolve_padded(): padded[:, 1 + offsets[0]:1 + offsets[0] + edge, 1 + offsets[1]:1 + offset...  19.7 us
    gather x26, other arithmetic  14.9 us
  transfers between devices with their start and end apart: 6, of which 0 were waited for; matrix products, arithmetic and copies ran while one was open for 21% of the time, Pallas kernels for 0%

commit v1 on v0

v1 whole, which is shorter than its diff:
```python
import jax
import jax.numpy as jnp
from jax import lax
from jax.experimental import pallas as pl
from jax.experimental.pallas import tpu as pltpu
from jax.sharding import PartitionSpec as P

CIN = 96
COUT = 48
EDGE = 16
PLANE = 256
VOX = 4096
SLOTS = 2
TAPS = 9
BF = jnp.bfloat16
F32 = jnp.float32

OWN_X = 0
FAR_X = 4
FAR_Y = 8
OWN_Y = 10
OWN_Z = 14
FAR_Z = 18
EDGE_Z = 22
EDGE_Y = 24
TURN_Z = 28
SOURCES = 32


def params(mib):
    return pltpu.CompilerParams(vmem_limit_bytes=mib * 2**20)


def lanes(rows, width):
    return lax.broadcasted_iota(jnp.int32, (rows, width), 1)


def last(side):
    return EDGE - 1 if side == 0 else 0


def roll(value, shift):
    width = value.shape[1]
    if isinstance(shift, int):
        shift = shift % width
        if shift == 0:
            return value
    return pltpu.roll(value, shift, 1)


def interior(block, wall, columns, write):
    lane = lanes(CIN, PLANE)
    z_of = lane % EDGE
    z_first, z_last = z_of == 0, z_of == EDGE - 1
    y_first, y_last = lane < EDGE, lane >= PLANE - EDGE
    zero = jnp.zeros((CIN, PLANE), BF)
    before = current = None
    for x in range(EDGE):
        centre = block(x)
        z_less = jnp.where(z_first, zero, roll(centre, 1))
        z_more = jnp.where(z_last, zero, roll(centre, -1))
        buffer = x % 2
        for tap_z, value in enumerate((z_less, centre, z_more)):
            for tap_y in range(3):
                if tap_y == 0:
                    shifted = jnp.where(y_first, zero, roll(value, EDGE))
                elif tap_y == 1:
                    shifted = value
                else:
                    shifted = jnp.where(y_last, zero, roll(value, -EDGE))
                start = (tap_y * 3 + tap_z) * CIN
                columns[buffer, start : start + CIN, :] = shifted
        part = jnp.dot(wall[...], columns[buffer], preferred_element_type=F32)
        if x > 0:
            write(x - 1, before + part[2 * COUT :])
            before = current + part[COUT : 2 * COUT]
        else:
            before = part[COUT : 2 * COUT]
        current = part[:COUT]
    write(EDGE - 1, before)


def write_plane(acc):
    def write(x, value):
        acc[:, x * PLANE : (x + 1) * PLANE] = value

    return write


def pack_and_convolve(blocks, weight, faces_y, faces_z, acc, wall, columns):
    for tap_x in range(3):
        wall[tap_x * COUT : (tap_x + 1) * COUT, :] = weight[
            :, tap_x * TAPS * CIN : (tap_x + 1) * TAPS * CIN
        ]
    lane = lanes(CIN, PLANE)
    half_lane = lanes(CIN, 128)
    for slot in range(SLOTS):
        for side in range(2):
            plane_z = jnp.zeros((CIN, PLANE), BF)
            halves = [jnp.zeros((CIN, 128), BF), jnp.zeros((CIN, 128), BF)]
            for x in range(EDGE):
                centre = blocks[slot, :, x * PLANE : (x + 1) * PLANE]
                plane_z = jnp.where(lane % EDGE == x, roll(centre, x - last(side)), plane_z)
                half = centre[:, 128:] if side == 0 else centre[:, :128]
                at = (x % 8) * EDGE
                moved = roll(half, at - (112 if side == 0 else 0))
                halves[x // 8] = jnp.where(half_lane // EDGE == x % 8, moved, halves[x // 8])
            faces_z[side * 2 + slot] = plane_z
            faces_y[side * 2 + slot, :, :128] = halves[0]
            faces_y[side * 2 + slot, :, 128:] = halves[1]
    interior(
        lambda x: blocks[0, :, x * PLANE : (x + 1) * PLANE], wall, columns, write_plane(acc)
    )


def convolve_second(blocks, wall, tie, acc, columns):
    interior(
        lambda x: blocks[0, :, x * PLANE : (x + 1) * PLANE], wall, columns, write_plane(acc)
    )


def pack_for_y(place, faces_y, far_a, far_b, out):
    odd_x, at_y = place[0] == 1, place[2]
    for slot in range(SLOTS):
        out[slot, :, :PLANE] = faces_y[at_y * 2 + slot]
        start = pl.multiple_of((1 - at_y) * 128, 128)
        a = far_a[slot, :, pl.ds(start, 128)]
        b = far_b[slot, :, pl.ds(start, 128)]
        out[slot, :, PLANE : PLANE + 128] = jnp.where(odd_x, a, b)
        out[slot, :, PLANE + 128 :] = jnp.where(odd_x, b, a)


def pack_for_z(place, faces_z, far_a, far_b, far_y, out_a, out_b):
    odd_x, odd_z, at_y = place[0] == 1, place[1] == 1, place[2]
    lane = lanes(CIN, PLANE)
    half_lane = lanes(CIN, 128)
    row = at_y * 112
    packs = []
    for side in range(2):
        z = last(side)
        pack = jnp.zeros((CIN, PLANE), BF)
        corner = jnp.zeros((CIN, 128), BF)
        for slot in range(SLOTS):
            a, b = far_a[slot], far_b[slot]
            pair = (jnp.where(odd_x, a, b), jnp.where(odd_x, b, a))
            for d in range(2):
                k = d * 2 + slot
                pack = jnp.where(lane % EDGE == k, roll(pair[d], k - z), pack)
                edge = far_y[slot, :, PLANE + d * 128 : PLANE + (d + 1) * 128]
                moved = pltpu.roll(edge, (6 + k - z - row) % 128, 1)
                corner = jnp.where(half_lane == 6 + k, moved, corner)
            k = 4 + slot
            pack = jnp.where(lane % EDGE == k, roll(far_y[slot, :, :PLANE], k - z), pack)
        low = jnp.where((half_lane >= 6) & (half_lane < 10), corner, pack[:, :128])
        packs.append((low, pack[:, 128:]))
    first, second = packs
    for part in range(2):
        at = slice(part * 128, (part + 1) * 128)
        out_a[2, :, at] = jnp.where(odd_z, second[part], first[part])
        out_b[2, :, at] = jnp.where(odd_z, first[part], second[part])
    for slot in range(SLOTS):
        out_a[slot] = faces_z[place[1] * 2 + slot]
        out_b[slot] = faces_z[(1 - place[1]) * 2 + slot]


def pick(code, choices):
    result = choices[-1][1]
    for known, value in reversed(choices[:-1]):
        result = jnp.where(code == known, value, result)
    return result


def finish(
    place, links, count, acc_a, acc_b, own_a, own_b, far_a, far_b, faces_y, far_y, faces_z,
    got_a, got_b, wall, bias, head, head_bias, turn, out, table, columns, extra
):
    odd_x, odd_z = place[0] == 1, place[1] == 1
    lane = lanes(CIN, PLANE)
    z_of = lane % EDGE
    z_first, z_last = z_of == 0, z_of == EDGE - 1
    y_first, y_last = lane < EDGE, lane >= PLANE - EDGE
    half_lane = lanes(CIN, 128)
    zero = jnp.zeros((CIN, PLANE), BF)
    half_zero = jnp.zeros((CIN, 128), BF)
    for slot in range(SLOTS):
        a, b = own_a[slot], own_b[slot]
        table[OWN_X + slot] = jnp.where(odd_x, b, a)
        table[OWN_X + 2 + slot] = jnp.where(odd_x, a, b)
        a, b = far_a[slot], far_b[slot]
        table[FAR_X + slot] = jnp.where(odd_x, a, b)
        table[FAR_X + 2 + slot] = jnp.where(odd_x, b, a)
        table[FAR_Y + slot] = far_y[slot, :, :PLANE]
        a, b = got_a[slot], got_b[slot]
        table[FAR_Z + slot] = jnp.where(odd_z, a, b)
        table[FAR_Z + 2 + slot] = jnp.where(odd_z, b, a)
        for d in range(2):
            table[OWN_Y + d * 2 + slot] = faces_y[d * 2 + slot]
            table[OWN_Z + d * 2 + slot] = faces_z[d * 2 + slot]
            table[EDGE_Y + d * 2 + slot, :, :128] = far_y[
                slot, :, PLANE + d * 128 : PLANE + (d + 1) * 128
            ]
            table[EDGE_Y + d * 2 + slot, :, 128:] = half_zero
    a, b = got_a[2], got_b[2]
    table[EDGE_Z] = jnp.where(odd_z, a, b)
    table[EDGE_Z + 1] = jnp.where(odd_z, b, a)
    for k in range(4):
        table[TURN_Z + k] = jnp.dot(
            table[FAR_Z + k], turn[...], preferred_element_type=F32
        ).astype(BF)

    def link(slot, dx, dy, dz):
        index = (dx + 1) * 9 + (dy + 1) * 3 + dz + 1
        value = links[slot, index if index < 13 else index - 1]
        clean = jnp.maximum(value, 0)
        return value >= 0, clean // 2, clean % 2

    def whole(present, index):
        return jnp.where(present, table[index], zero)

    def column(present, index, source, side):
        target = 0 if side == 0 else EDGE - 1
        moved = pltpu.roll(table[index], (target - source + PLANE) % PLANE, 1)
        return jnp.where(present, moved, zero)

    def short(present, index, source, target):
        start = pl.multiple_of((source // 128) * 128, 128)
        value = table[index, :, pl.ds(start, 128)]
        moved = pltpu.roll(value, (target - source % 128 + 128) % 128, 1)
        return jnp.where(present, moved, half_zero)

    def sign(side):
        return -1 if side == 0 else 1

    accs = (acc_a, acc_b)
    lane_o = lanes(COUT, PLANE)
    half_o = lanes(COUT, 128)
    none = jnp.zeros((COUT, PLANE), F32)
    for slot in range(SLOTS):
        acc = accs[slot]
        for d in range(2):
            present, code, u = link(slot, sign(d), 0, 0)
            centre = whole(present, code * 4 + d * 2 + u)
            sides = []
            for f in range(2):
                present, code, u = link(slot, sign(d), 0, sign(f))
                index = pick(
                    code,
                    (
                        (0, d * 2 + u),
                        (1, FAR_X + d * 2 + u),
                        (4, FAR_Z + f * 2 + u),
                        (5, EDGE_Z + f),
                    ),
                )
                source = pick(code, ((0, last(f)), (1, last(f)), (4, last(d)), (5, d * 2 + u)))
                sides.append(column(present, index, source, f))
            z_less = jnp.where(z_first, sides[0], roll(centre, 1))
            z_more = jnp.where(z_last, sides[1], roll(centre, -1))
            rows = []
            for e in range(2):
                present, code, u = link(slot, sign(d), sign(e), 0)
                index = pick(
                    code,
                    (
                        (0, d * 2 + u),
                        (1, FAR_X + d * 2 + u),
                        (2, FAR_Y + u),
                        (3, EDGE_Y + d * 2 + u),
                    ),
                )
                far = 112 if e == 0 else 0
                source = pick(
                    code,
                    ((0, last(e) * EDGE), (1, last(e) * EDGE), (2, last(d) * EDGE), (3, far)),
                )
                row = short(present, index, source, 0)
                for f in range(2):
                    present, code, u = link(slot, sign(d), sign(e), sign(f))
                    index = pick(
                        code,
                        (
                            (0, d * 2 + u),
                            (1, FAR_X + d * 2 + u),
                            (2, FAR_Y + u),
                            (3, EDGE_Y + d * 2 + u),
                            (4, FAR_Z + f * 2 + u),
                            (5, EDGE_Z + f),
                        ),
                    )
                    source = pick(
                        code,
                        (
                            (0, last(e) * EDGE + last(f)),
                            (1, last(e) * EDGE + last(f)),
                            (2, last(d) * EDGE + last(f)),
                            (3, far + last(f)),
                            (4, last(e) * EDGE + last(d)),
                            (5, last(e) * EDGE + d * 2 + u),
                            (6, last(d) * EDGE + 4 + u),
                            (7, 6 + d * 2 + u),
                        ),
                    )
                    target = 127 if f == 0 else EDGE
                    row = jnp.where(half_lane == target, short(present, index, source, target), row)
                rows.append(row)
            for tap_z, value in enumerate((z_less, centre, z_more)):
                low, high = roll(rows[0], 1 - tap_z), roll(rows[1], 1 - tap_z)
                for tap_y in range(3):
                    start = (tap_y * 3 + tap_z) * CIN
                    if tap_y == 1:
                        columns[d, start : start + CIN, :] = value
                    elif tap_y == 0:
                        shifted = roll(value, EDGE)
                        columns[d, start : start + CIN, :128] = jnp.where(
                            half_lane < EDGE, low, shifted[:, :128]
                        )
                        columns[d, start : start + CIN, 128:] = shifted[:, 128:]
                    else:
                        shifted = roll(value, -EDGE)
                        columns[d, start : start + CIN, :128] = shifted[:, :128]
                        columns[d, start : start + CIN, 128:] = jnp.where(
                            half_lane >= 112, roll(high, 112), shifted[:, 128:]
                        )
            x = 0 if d == 0 else EDGE - 1
            at = slice(x * PLANE, (x + 1) * PLANE)
            taps = wall[2 * d * COUT : (2 * d + 1) * COUT, :]
            extra[:, at] = acc[:, at] + jnp.dot(taps, columns[d], preferred_element_type=F32)
        sheets_y = []
        for e in range(2):
            present, code, u = link(slot, 0, sign(e), 0)
            centre = whole(present, pick(code, ((0, OWN_Y + e * 2 + u), (2, FAR_Y + u))))
            sides = []
            for f in range(2):
                present, code, u = link(slot, 0, sign(e), sign(f))
                index = pick(
                    code,
                    (
                        (0, OWN_Y + e * 2 + u),
                        (2, FAR_Y + u),
                        (4, TURN_Z + f * 2 + u),
                        (6, EDGE_Z + f),
                    ),
                )
                source = pick(code, ((0, last(f)), (2, last(f)), (4, last(e)), (6, 4 + u)))
                sides.append(column(present, index, source, f))
            columns[e, :CIN, :] = jnp.where(z_first, sides[0], roll(centre, 1))
            columns[e, CIN : 2 * CIN, :] = centre
            columns[e, 2 * CIN : 3 * CIN, :] = jnp.where(z_last, sides[1], roll(centre, -1))
            taps = wall[:, 2 * e * 3 * CIN : (2 * e + 1) * 3 * CIN]
            part = jnp.dot(taps, columns[e, : 3 * CIN, :], preferred_element_type=F32)
            sheet = part[COUT : 2 * COUT]
            sheet = sheet + jnp.where(lane_o < EDGE, none, roll(part[:COUT], EDGE))
            sheet = sheet + jnp.where(
                lane_o >= PLANE - EDGE, none, roll(part[2 * COUT :], -EDGE)
            )
            sheets_y.append(sheet)
        sheets_z = []
        for f in range(2):
            present, code, u = link(slot, 0, 0, sign(f))
            centre = whole(present, pick(code, ((0, OWN_Z + f * 2 + u), (4, FAR_Z + f * 2 + u))))
            part = jnp.zeros((3 * COUT, PLANE), F32)
            for tap_y in range(3):
                if tap_y == 0:
                    value = jnp.where(y_first, zero, roll(centre, EDGE))
                elif tap_y == 1:
                    value = centre
                else:
                    value = jnp.where(y_last, zero, roll(centre, -EDGE))
                columns[f, tap_y * CIN : (tap_y + 1) * CIN, :] = value
            taps = jnp.concatenate(
                [
                    wall[:, (tap_y * 3 + 2 * f) * CIN : (tap_y * 3 + 2 * f + 1) * CIN]
                    for tap_y in range(3)
                ],
                1,
            )
            part = jnp.dot(taps, columns[f, : 3 * CIN, :], preferred_element_type=F32)
            sheet = part[COUT : 2 * COUT]
            sheet = sheet + jnp.where(lane_o % EDGE == 0, none, roll(part[:COUT], 1))
            sheet = sheet + jnp.where(
                lane_o % EDGE == EDGE - 1, none, roll(part[2 * COUT :], -1)
            )
            sheets_z.append(sheet)
        used = slot < count[0]
        half_none = jnp.zeros((COUT, 128), F32)
        for x in range(EDGE):
            at = slice(x * PLANE, (x + 1) * PLANE)
            total = extra[:, at] if x in (0, EDGE - 1) else acc[:, at]
            total = total + jnp.where(lane_o % EDGE == 0, roll(sheets_z[0], -x), none)
            total = total + jnp.where(
                lane_o % EDGE == EDGE - 1, roll(sheets_z[1], EDGE - 1 - x), none
            )
            from_half = slice((x // 8) * 128, (x // 8 + 1) * 128)
            low = roll(sheets_y[0][:, from_half], -(x % 8) * EDGE)
            high = roll(sheets_y[1][:, from_half], 112 - (x % 8) * EDGE)
            low = total[:, :128] + jnp.where(half_o < EDGE, low, half_none)
            high = total[:, 128:] + jnp.where(half_o >= 112, high, half_none)
            for part, value in enumerate((low, high)):
                hidden = jnp.maximum(value + bias[...], 0.0).astype(BF)
                mixed = jnp.dot(head[...], hidden, preferred_element_type=F32) + head_bias[...]
                out[slot, :, x * PLANE + part * 128 : x * PLANE + (part + 1) * 128] = jnp.where(
                    used, mixed, half_none
                ).astype(BF)


SMEM = pl.BlockSpec(memory_space=pltpu.SMEM)
VMEM = pl.BlockSpec(memory_space=pltpu.VMEM)


def shape(dims, kind=BF):
    return jax.ShapeDtypeStruct(dims, kind)


def swap(first, second, axis):
    length = lax.axis_size(axis)
    even = [(i, i ^ 1) for i in range(length)]
    odd = [(i, ((i + 1) ^ 1) - 1) for i in range(1, length - 1)]
    return lax.ppermute(first, axis, even), lax.ppermute(second, axis, odd)


def body(blocks, block_count, neighbours, conv_weight, conv_bias, head_weight, head_bias):
    volumes = blocks.reshape(SLOTS, CIN, VOX)
    count = block_count.reshape(1)
    links = neighbours.reshape(SLOTS, 26)
    odd_x = lax.axis_index("gx") % 2
    odd_z = lax.axis_index("gz") % 2
    place = jnp.stack([odd_x, odd_z, lax.axis_index("gy")]).astype(jnp.int32)
    far_end = VOX - PLANE
    own_a = lax.dynamic_slice_in_dim(volumes, (1 - odd_x) * far_end, PLANE, 2)
    own_b = lax.dynamic_slice_in_dim(volumes, odd_x * far_end, PLANE, 2)
    far_a, far_b = swap(own_a, own_b, "gx")
    buffer = pltpu.VMEM((2, TAPS * CIN, PLANE), BF)
    faces_y, faces_z, acc_a, wall = pl.pallas_call(
        pack_and_convolve,
        out_shape=(
            shape((4, CIN, PLANE)),
            shape((4, CIN, PLANE)),
            shape((COUT, VOX), F32),
            shape((3 * COUT, TAPS * CIN)),
        ),
        in_specs=[VMEM, VMEM],
        out_specs=(VMEM, VMEM, VMEM, VMEM),
        scratch_shapes=[buffer],
        compiler_params=params(16),
        cost_estimate=pl.CostEstimate(
            flops=2 * COUT * 27 * CIN * VOX, bytes_accessed=4 * 2**20, transcendentals=0
        ),
    )(volumes, conv_weight)
    sent_y = pl.pallas_call(
        pack_for_y,
        out_shape=shape((SLOTS, CIN, 2 * PLANE)),
        in_specs=[SMEM, VMEM, VMEM, VMEM],
        out_specs=VMEM,
        compiler_params=params(8),
    )(place, faces_y, far_a, far_b)
    far_y = lax.ppermute(sent_y, "gy", [(0, 1), (1, 0)])
    sent_a, sent_b = pl.pallas_call(
        pack_for_z,
        out_shape=(shape((3, CIN, PLANE)), shape((3, CIN, PLANE))),
        in_specs=[SMEM, VMEM, VMEM, VMEM, VMEM],
        out_specs=(VMEM, VMEM),
        compiler_params=params(8),
    )(place, faces_z, far_a, far_b, far_y)
    got_a, got_b = swap(sent_a, sent_b, "gz")
    acc_b = pl.pallas_call(
        convolve_second,
        grid=(1,),
        out_shape=shape((COUT, VOX), F32),
        in_specs=[
            pl.BlockSpec((1, CIN, VOX), lambda i: (1, 0, 0)),
            VMEM,
            pl.BlockSpec(memory_space=pl.ANY),
        ],
        out_specs=VMEM,
        scratch_shapes=[buffer],
        compiler_params=params(16),
        cost_estimate=pl.CostEstimate(
            flops=2 * COUT * 27 * CIN * VOX, bytes_accessed=2 * 2**20, transcendentals=0
        ),
    )(volumes, wall, sent_a)
    index = jnp.arange(PLANE)
    turn = (index[:, None] == (index % EDGE * EDGE + index // EDGE)[None, :]).astype(BF)
    outputs = pl.pallas_call(
        finish,
        out_shape=shape((SLOTS, COUT, VOX)),
        in_specs=[SMEM] * 3 + [VMEM] * 16,
        out_specs=VMEM,
        scratch_shapes=[
            pltpu.VMEM((SOURCES, CIN, PLANE), BF),
            buffer,
            pltpu.VMEM((COUT, VOX), F32),
        ],
        compiler_params=params(24),
    )(
        place, links, count, acc_a, acc_b, own_a, own_b, far_a, far_b, faces_y, far_y, faces_z,
        got_a, got_b, wall, conv_bias.reshape(COUT, 1), head_weight,
        head_bias.reshape(COUT, 1), turn,
    )
    return outputs.reshape(1, 1, SLOTS, COUT, VOX)


def solution(mesh):
    placed = (
        P("gx", "gz", "gy", None, None),
        P("gx", "gz", "gy"),
        P("gx", "gz", "gy", None),
        P(),
        P(),
        P(),
        P(),
    )
    return jax.shard_map(
        body, mesh=mesh, in_specs=placed, out_specs=P("gx", "gz", "gy", None, None), check_vma=False
    )
```

time: 398 us -> 35.1 us (0.09)
  the two profiles are of different devices: /device:TPU:103 before, /device:TPU:78 now
where the time goes in v1:
time: 35.1 us; the launch traced here: 34.9 us
  Pallas kernels  14.6 us (42%)
  starting transfers between devices  13 us (37%)
  local copies, waits for them, and re-layouts  4.92 us (14%)
  waiting for transfers between devices  1.43 us (4%)
  between operations  0.78 us (2%)
    ppermute x4, starting transfers between devices, swap(): return (lax.ppermute(first, axis, even), lax.ppermute(second, axis, odd))  13 us
    pallas_call x1, Pallas kernels, body(): pl.pallas_call(finish, out_shape=shape((SLOTS, COUT, VOX)), in_specs=[SME...  6.98 us
    unnamed x14, local copies, waits for them, and re-layouts  3.78 us
    pallas_call x1, Pallas kernels, body(): pl.pallas_call(pack_and_convolve, out_shape=(shape((4, CIN, PLANE)), shap...  3.77 us
    pallas_call x1, Pallas kernels, body(): pl.pallas_call(convolve_second, grid=(1,), out_shape=shape((COUT, VOX), F...  2.44 us
    ppermute x1, waiting for transfers between devices, body(): far_y = lax.ppermute(sent_y, 'gy', [(0, 1), (1, 0)])  1.42 us
    dynamic_slice x1, local copies, waits for them, and re-layouts, body(): own_b = lax.dynamic_slice_in_dim(volumes, odd_x * far_end, PLANE, 2)  0.95 us
    pallas_call x1, Pallas kernels, body(): pl.pallas_call(pack_for_z, out_shape=(shape((3, CIN, PLANE)), shape((3, C...  0.81 us
  transfers between devices with their start and end apart: 5, of which 1 were waited for; matrix products, arithmetic and copies ran while one was open for 1% of the time, Pallas kernels for 18%

profile of v1, /device:TPU:78, one launch (start us, length us, event | category | flops | bytes accessed | tf_op | source)
XLA Modules:
  0.0 34.9 jit_solution(13246191733933529987)
XLA Ops:
  0.0 1.0 %dynamic-slice_bitcast_fusion = (bf16[2,96,256]{2,1,0:T(8,128)(2,1)S(1)}, bf16[2,96,256]{2,1,0:T(8,128)(2,1)S(1)}) fusion(bf16[1,1,2,96,4096]{4,3,2,1,0:T(8,128)(2,1)} %param.7, s32[]{:T(128)S(6)} %select_n.39, s32[]{:T(128)S(6)} %select_n.38), kind=kLoop, calls=%fused_computation.2 | loop fusion | bytes 393224 | tf_op jit(solution)/shard_map/dynamic_slice | solution.py:430
  1.0 3.5 %collective-permute-start.1 = (bf16[2,96,256]{2,1,0:T(8,128)(2,1)S(1)}, bf16[2,96,256]{2,1,0:T(8,128)(2,1)S(1)}, u32[]{:S(2)}, u32[]{:S(2)}) collective-permute-start(bf16[2,96,256]{2,1,0:T(8,128)(2,1)S(1)} %get-tuple-element.17.own_b), channel_id=1, source_target_pairs={{16,32},{32,16},{48,64},{64,48},{80,96},{96,80},{112,128},{128,112... | collective-permute-start | bytes 294920 | tf_op jit(solution)/shard_map/ppermute | solution.py:418
  4.5 2.2 %collective-permute-start = (bf16[2,96,256]{2,1,0:T(8,128)(2,1)S(1)}, bf16[2,96,256]{2,1,0:T(8,128)(2,1)S(1)}, u32[]{:S(2)}, u32[]{:S(2)}) collective-permute-start(bf16[2,96,256]{2,1,0:T(8,128)(2,1)S(1)} %get-tuple-element.18.own_a), channel_id=1, source_target_pairs={{0,16},{16,0},{32,48},{48,32},{64,80},{80,64},{96,112},{112,96},{1... | collective-permute-start | bytes 294920 | tf_op jit(solution)/shard_map/ppermute | solution.py:418
  6.7 0.1 pad_add_fusion.place
  6.8 0.0 copy-start
  6.8 1.4 %copy-done = bf16[1,1,2,96,4096]{4,3,2,1,0:T(8,128)(2,1)S(1)} copy-done((bf16[1,1,2,96,4096]{4,3,2,1,0:T(8,128)(2,1)S(1)}, bf16[1,1,2,96,4096]{4,3,2,1,0:T(8,128)(2,1)}, u32[]{:S(2)}) %copy-start) | copy-done | bytes 1572888
  8.2 0.0 copy-start.4
  8.2 0.9 %copy-done.4 = bf16[48,2592]{1,0:T(8,128)(2,1)S(1)} copy-done((bf16[48,2592]{1,0:T(8,128)(2,1)S(1)}, bf16[48,2592]{1,0:T(8,128)(2,1)}, u32[]{:S(2)}) %copy-start.4) | copy-done | bytes 248856
  9.1 0.0 copy-start.5
  9.1 0.0 copy-start.6
  9.1 3.8 %shard_map.73 = (bf16[4,96,256]{2,1,0:T(8,128)(2,1)S(1)}, bf16[4,96,256]{2,1,0:T(8,128)(2,1)S(1)}, f32[48,4096]{1,0:T(8,128)S(1)}, bf16[144,864]{1,0:T(8,128)(2,1)S(1)}) custom-call(bf16[2,96,4096]{2,1,0:T(8,128)(2,1)S(1)} %bitcast.14, bf16[48,2592]{1,0:T(8,128)(2,1)S(1)} %copy-done.4), custom_call_target="tpu_custom_call" | custom-call | flops 1019215872 | bytes 4194304 | tf_op jit(solution)/shard_map/pallas_call | solution.py:433
  12.9 0.0 collective-permute-done.1.far_b
  12.9 0.0 collective-permute-done.far_a
  12.9 0.6 %shard_map.74 = bf16[2,96,512]{2,1,0:T(8,128)(2,1)S(1)} custom-call(s32[3]{0:T(128)S(1)} %pad_add_fusion.place, bf16[4,96,256]{2,1,0:T(8,128)(2,1)S(1)} %get-tuple-element.14.faces_y, bf16[2,96,256]{2,1,0:T(8,128)(2,1)S(1)} %collective-permute-done.far_a, bf16[2,96,256]{2,1,0:T(8,128)(2,1)S(1)} %collective-permute-done.1.far_b), custom_call_target="tpu_custom_call" | custom-call | tf_op jit(solution)/shard_map/pallas_call | solution.py:449
  13.5 0.1 collective-permute-start.2
  13.6 1.4 %collective-permute-done.2.far_y = bf16[2,96,512]{2,1,0:T(8,128)(2,1)S(1)} collective-permute-done((bf16[2,96,512]{2,1,0:T(8,128)(2,1)S(1)}, bf16[2,96,512]{2,1,0:T(8,128)(2,1)S(1)}, u32[]{:S(2)}, u32[]{:S(2)}) %collective-permute-start.2) | collective-permute-done | bytes 196640 | tf_op jit(solution)/shard_map/ppermute | solution.py:456
  15.0 0.8 %shard_map.75 = (bf16[3,96,256]{2,1,0:T(8,128)(2,1)S(1)}, bf16[3,96,256]{2,1,0:T(8,128)(2,1)S(1)}) custom-call(s32[3]{0:T(128)S(1)} %pad_add_fusion.place, bf16[4,96,256]{2,1,0:T(8,128)(2,1)S(1)} %get-tuple-element.13.faces_z, bf16[2,96,256]{2,1,0:T(8,128)(2,1)S(1)} %collective-permute-done.far_a, bf16[2,96,256]{2,1,0:T(8,128)(2,1)S(1)} %collective-permute-done.1.far_b, ...), custom_call_target="tpu_custom_call" | custom-call | tf_op jit(solution)/shard_map/pallas_call | solution.py:457
  15.9 2.0 %collective-permute-start.4 = (bf16[3,96,256]{2,1,0:T(8,128)(2,1)S(1)}, bf16[3,96,256]{2,1,0:T(8,128)(2,1)S(1)}, u32[]{:S(2)}, u32[]{:S(2)}) collective-permute-start(bf16[3,96,256]{2,1,0:T(8,128)(2,1)S(1)} %get-tuple-element.16), channel_id=1, source_target_pairs={{2,4},{4,2},{6,8},{8,6},{10,12},{12,10},{3,5},{5,3},{7,9},{9,7},{1... | collective-permute-start | bytes 442376 | tf_op jit(solution)/shard_map/ppermute | solution.py:418
  17.9 5.2 %collective-permute-start.3 = (bf16[3,96,256]{2,1,0:T(8,128)(2,1)S(1)}, bf16[3,96,256]{2,1,0:T(8,128)(2,1)S(1)}, u32[]{:S(2)}, u32[]{:S(2)}) collective-permute-start(bf16[3,96,256]{2,1,0:T(8,128)(2,1)S(1)} %get-tuple-element.15.tie), channel_id=1, source_target_pairs={{0,2},{2,0},{4,6},{6,4},{8,10},{10,8},{12,14},{14,12},{1,3},{3,1},... | collective-permute-start | bytes 442376 | tf_op jit(solution)/shard_map/ppermute | solution.py:418
  23.8 0.0 copy-done.5
  23.8 0.1 copy.8.bias
  23.9 0.0 copy-done.6
  23.9 0.1 copy.9.head_bias
  24.0 0.0 copy-start.1
  24.0 1.4 %copy-done.1 = bf16[1,1,2,96,4096]{4,3,2,1,0:T(8,128)(2,1)S(1)} copy-done((bf16[1,1,2,96,4096]{4,3,2,1,0:T(8,128)(2,1)S(1)}, bf16[1,1,2,96,4096]{4,3,2,1,0:T(8,128)(2,1)}, u32[]{:S(2)}) %copy-start.1) | copy-done | bytes 1572888
  25.4 0.0 copy-start.2
  25.4 0.0 copy-start.3
  25.4 2.4 %shard_map.76.acc_b = f32[48,4096]{1,0:T(8,128)S(1)} custom-call(bf16[2,96,4096]{2,1,0:T(8,128)(2,1)S(1)} %bitcast.15, bf16[144,864]{1,0:T(8,128)(2,1)S(1)} %get-tuple-element.12.wall, bf16[3,96,256]{2,1,0:T(8,128)(2,1)S(1)} %get-tuple-element.15.tie), custom_call_target="tpu_custom_call" | custom-call | flops 1019215872 | bytes 2097152 | tf_op jit(solution)/shard_map/pallas_call | solution.py:465
  27.8 0.0 collective-permute-done.4.got_b
  27.9 0.0 collective-permute-done.3.got_a
  27.9 0.0 copy-done.2
  27.9 0.0 copy-done.3
  27.9 7.0 %shard_map.77 = bf16[2,48,4096]{2,1,0:T(8,128)(2,1)} custom-call(s32[3]{0:T(128)S(1)} %pad_add_fusion.place, s32[2,26]{1,0:T(2,128)S(1)} %bitcast.16, s32[1]{0:T(128)} %bitcast.13.count, f32[48,4096]{1,0:T(8,128)S(1)} %get-tuple-element.11.acc_a, f32[48,4096]{1,0:T(8,128)S(1)} %shard_map.76.acc_b, bf16[2,96,256]{2,1,0:T(8,128)(2,1)S(1)} %get-tuple-element.18.own_a, ...), custom_call_target="tpu_custom_call" | custom-call | tf_op jit(solution)/shard_map/pallas_call | solution.py:483
  (2 shorter events, 0.0 us)
Async XLA Ops:
  1.0 12.0 %collective-permute-start.1 = (bf16[2,96,256]{2,1,0:T(8,128)(2,1)S(1)}, bf16[2,96,256]{2,1,0:T(8,128)(2,1)S(1)}, u32[]{:S(2)}, u32[]{:S(2)}) collective-permute-start(bf16[2,96,256]{2,1,0:T(8,128)(2,1)S(1)} %get-tuple-element.17.own_b), channel_id=1, source_target_pairs={{16,32},{32,16},{48,64},{64,48},{80,96},{96,80},{112,128},{128,112... | collective-permute-start | bytes 294920 | tf_op jit(solution)/shard_map/ppermute | solution.py:418
  4.5 8.5 %collective-permute-start = (bf16[2,96,256]{2,1,0:T(8,128)(2,1)S(1)}, bf16[2,96,256]{2,1,0:T(8,128)(2,1)S(1)}, u32[]{:S(2)}, u32[]{:S(2)}) collective-permute-start(bf16[2,96,256]{2,1,0:T(8,128)(2,1)S(1)} %get-tuple-element.18.own_a), channel_id=1, source_target_pairs={{0,16},{16,0},{32,48},{48,32},{64,80},{80,64},{96,112},{112,96},{1... | collective-permute-start | bytes 294920 | tf_op jit(solution)/shard_map/ppermute | solution.py:418
  6.8 1.4 %copy-start = (bf16[1,1,2,96,4096]{4,3,2,1,0:T(8,128)(2,1)S(1)}, bf16[1,1,2,96,4096]{4,3,2,1,0:T(8,128)(2,1)}, u32[]{:S(2)}) copy-start(bf16[1,1,2,96,4096]{4,3,2,1,0:T(8,128)(2,1)} %param.7) | copy-start | bytes 4718596
  8.2 0.9 %copy-start.4 = (bf16[48,2592]{1,0:T(8,128)(2,1)S(1)}, bf16[48,2592]{1,0:T(8,128)(2,1)}, u32[]{:S(2)}) copy-start(bf16[48,2592]{1,0:T(8,128)(2,1)} %weight.1) | copy-start | bytes 746500
  9.1 14.7 %copy-start.5 = (f32[48]{0:T(128)S(1)}, f32[48]{0:T(128)}, u32[]{:S(2)}) copy-start(f32[48]{0:T(128)} %param.11) | copy-start | bytes 580
  9.1 14.8 %copy-start.6 = (f32[48]{0:T(128)S(1)}, f32[48]{0:T(128)}, u32[]{:S(2)}) copy-start(f32[48]{0:T(128)} %param.13) | copy-start | bytes 580
  13.5 1.5 %collective-permute-start.2 = (bf16[2,96,512]{2,1,0:T(8,128)(2,1)S(1)}, bf16[2,96,512]{2,1,0:T(8,128)(2,1)S(1)}, u32[]{:S(2)}, u32[]{:S(2)}) collective-permute-start(bf16[2,96,512]{2,1,0:T(8,128)(2,1)S(1)} %shard_map.74), channel_id=1, source_target_pairs={{0,1},{1,0},{2,3},{3,2},{4,5},{5,4},{6,7},{7,6},{8,9},{9,8},{10,11... | collective-permute-start | bytes 589832 | tf_op jit(solution)/shard_map/ppermute | solution.py:456
  15.9 12.0 %collective-permute-start.4 = (bf16[3,96,256]{2,1,0:T(8,128)(2,1)S(1)}, bf16[3,96,256]{2,1,0:T(8,128)(2,1)S(1)}, u32[]{:S(2)}, u32[]{:S(2)}) collective-permute-start(bf16[3,96,256]{2,1,0:T(8,128)(2,1)S(1)} %get-tuple-element.16), channel_id=1, source_target_pairs={{2,4},{4,2},{6,8},{8,6},{10,12},{12,10},{3,5},{5,3},{7,9},{9,7},{1... | collective-permute-start | bytes 442376 | tf_op jit(solution)/shard_map/ppermute | solution.py:418
  17.9 10.0 %collective-permute-start.3 = (bf16[3,96,256]{2,1,0:T(8,128)(2,1)S(1)}, bf16[3,96,256]{2,1,0:T(8,128)(2,1)S(1)}, u32[]{:S(2)}, u32[]{:S(2)}) collective-permute-start(bf16[3,96,256]{2,1,0:T(8,128)(2,1)S(1)} %get-tuple-element.15.tie), channel_id=1, source_target_pairs={{0,2},{2,0},{4,6},{6,4},{8,10},{10,8},{12,14},{14,12},{1,3},{3,1},... | collective-permute-start | bytes 442376 | tf_op jit(solution)/shard_map/ppermute | solution.py:418
  24.0 1.4 %copy-start.1 = (bf16[1,1,2,96,4096]{4,3,2,1,0:T(8,128)(2,1)S(1)}, bf16[1,1,2,96,4096]{4,3,2,1,0:T(8,128)(2,1)}, u32[]{:S(2)}) copy-start(bf16[1,1,2,96,4096]{4,3,2,1,0:T(8,128)(2,1)} %param.7) | copy-start | bytes 4718596
  25.4 2.5 %copy-start.2 = (bf16[48,48]{1,0:T(8,128)(2,1)S(1)}, bf16[48,48]{1,0:T(8,128)(2,1)}, u32[]{:S(2)}) copy-start(bf16[48,48]{1,0:T(8,128)(2,1)} %head.1) | copy-start | bytes 13828
  25.4 2.5 %copy-start.3 = (s32[1,1,2,26]{3,2,1,0:T(2,128)S(1)}, s32[1,1,2,26]{3,2,1,0:T(2,128)}, u32[]{:S(2)}) copy-start(s32[1,1,2,26]{3,2,1,0:T(2,128)} %param.9) | copy-start | bytes 628

commit v2 on v1

v2 whole, which is shorter than its diff:
```python
import jax
import jax.numpy as jnp
from jax import lax
from jax.experimental import pallas as pl
from jax.experimental.pallas import tpu as pltpu
from jax.sharding import PartitionSpec as P

CIN = 96
COUT = 48
EDGE = 16
PLANE = 256
VOX = 4096
SLOTS = 2
TAPS = 9
BF = jnp.bfloat16
F32 = jnp.float32

OWN_X, FAR_X, FAR_Y, OWN_Y, EDGE_Y, NEAR_SOURCES = 0, 4, 8, 10, 14, 18
FAR_Z, EDGE_Z, TURN_Z, Z_SOURCES = 0, 4, 6, 8
SPLIT = 5
CHUNK = 4


def params(mib):
    return pltpu.CompilerParams(vmem_limit_bytes=mib * 2**20)


def lanes(rows, width):
    return lax.broadcasted_iota(jnp.int32, (rows, width), 1)


def last(side):
    return EDGE - 1 if side == 0 else 0


def roll(value, shift):
    width = value.shape[1]
    if isinstance(shift, int):
        shift = shift % width
        if shift == 0:
            return value
    return pltpu.roll(value, shift, 1)


def place():
    return lax.axis_index("gx") % 2, lax.axis_index("gz") % 2, lax.axis_index("gy")


def interior(block, wall, columns, write, first, stop, carry=None):
    lane = lanes(CIN, PLANE)
    z_of = lane % EDGE
    z_first, z_last = z_of == 0, z_of == EDGE - 1
    y_first, y_last = lane < EDGE, lane >= PLANE - EDGE
    zero = jnp.zeros((CIN, PLANE), BF)
    before, current = carry if carry is not None else (None, None)
    for x in range(first, stop):
        centre = block(x)
        z_less = jnp.where(z_first, zero, roll(centre, 1))
        z_more = jnp.where(z_last, zero, roll(centre, -1))
        buffer = x % 2
        for tap_z, value in enumerate((z_less, centre, z_more)):
            for tap_y in range(3):
                if tap_y == 0:
                    shifted = jnp.where(y_first, zero, roll(value, EDGE))
                elif tap_y == 1:
                    shifted = value
                else:
                    shifted = jnp.where(y_last, zero, roll(value, -EDGE))
                start = (tap_y * 3 + tap_z) * CIN
                columns[buffer, start : start + CIN, :] = shifted
        part = jnp.dot(wall[...], columns[buffer], preferred_element_type=F32)
        if x > 0:
            write(x - 1, before + part[2 * COUT :])
            before = current + part[COUT : 2 * COUT]
        else:
            before = part[COUT : 2 * COUT]
        current = part[:COUT]
    if stop == EDGE:
        write(EDGE - 1, before)
    return before, current


def write_plane(acc):
    def write(x, value):
        acc[:, x * PLANE : (x + 1) * PLANE] = value

    return write


def plane_of(block):
    return lambda x: block[:, x * PLANE : (x + 1) * PLANE]


def pack_and_convolve(blocks, weight, held, faces_y, faces_z, acc, wall, columns, first, weights, sems, weight_sem):
    width = VOX // CHUNK
    copies = []
    for slot in range(SLOTS):
        for part in range(CHUNK):
            at = pl.ds(part * width, width)
            copies.append(
                pltpu.make_async_copy(
                    blocks.at[slot, :, at], (first, held)[slot].at[:, at], sems.at[slot * CHUNK + part]
                )
            )
    weight_copy = pltpu.make_async_copy(weight, weights, weight_sem)
    copies[0].start()
    weight_copy.start()
    for copy in copies[1:]:
        copy.start()
    lane = lanes(CIN, PLANE)
    half_lane = lanes(CIN, 128)
    for slot in range(SLOTS):
        planes_z = [jnp.zeros((CIN, PLANE), BF)] * 2
        halves = [[jnp.zeros((CIN, 128), BF)] * 2 for _ in range(2)]
        for x in range(EDGE):
            if x % (EDGE // CHUNK) == 0:
                copies[slot * CHUNK + x // (EDGE // CHUNK)].wait()
            centre = (first, held)[slot][:, x * PLANE : (x + 1) * PLANE]
            for side in range(2):
                planes_z[side] = jnp.where(
                    lane % EDGE == x, roll(centre, x - last(side)), planes_z[side]
                )
                half = centre[:, 128:] if side == 0 else centre[:, :128]
                at = (x % 8) * EDGE
                moved = roll(half, at - (112 if side == 0 else 0))
                halves[side][x // 8] = jnp.where(
                    half_lane // EDGE == x % 8, moved, halves[side][x // 8]
                )
        for side in range(2):
            faces_z[side * 2 + slot] = planes_z[side]
            faces_y[side * 2 + slot, :, :128] = halves[side][0]
            faces_y[side * 2 + slot, :, 128:] = halves[side][1]
        if slot == 0:
            weight_copy.wait()
            for tap_x in range(3):
                wall[tap_x * COUT : (tap_x + 1) * COUT, :] = weights[
                    :, tap_x * TAPS * CIN : (tap_x + 1) * TAPS * CIN
                ]
            interior(plane_of(first), wall, columns, write_plane(acc), 0, EDGE)


def begin_second(held, wall, tie, acc, carry, columns):
    before, current = interior(plane_of(held), wall, columns, write_plane(acc), 0, SPLIT)
    carry[0], carry[1] = before, current


def pack_for_y(faces_y, far_a, far_b, out):
    parity, _, at_y = place()
    odd_x = parity == 1
    for slot in range(SLOTS):
        out[slot, :, :PLANE] = faces_y[at_y * 2 + slot]
        start = pl.multiple_of((1 - at_y) * 128, 128)
        a = far_a[slot, :, pl.ds(start, 128)]
        b = far_b[slot, :, pl.ds(start, 128)]
        out[slot, :, PLANE : PLANE + 128] = jnp.where(odd_x, a, b)
        out[slot, :, PLANE + 128 :] = jnp.where(odd_x, b, a)


def pack_for_z(faces_z, far_a, far_b, far_y, out_a, out_b):
    parity_x, parity_z, at_y = place()
    odd_x, odd_z = parity_x == 1, parity_z == 1
    lane = lanes(CIN, PLANE)
    half_lane = lanes(CIN, 128)
    row = at_y * 112
    packs = []
    for side in range(2):
        z = last(side)
        pack = jnp.zeros((CIN, PLANE), BF)
        corner = jnp.zeros((CIN, 128), BF)
        for slot in range(SLOTS):
            a, b = far_a[slot], far_b[slot]
            pair = (jnp.where(odd_x, a, b), jnp.where(odd_x, b, a))
            for d in range(2):
                k = d * 2 + slot
                pack = jnp.where(lane % EDGE == k, roll(pair[d], k - z), pack)
                edge = far_y[slot, :, PLANE + d * 128 : PLANE + (d + 1) * 128]
                moved = pltpu.roll(edge, (6 + k - z - row + 128) % 128, 1)
                corner = jnp.where(half_lane == 6 + k, moved, corner)
            k = 4 + slot
            pack = jnp.where(lane % EDGE == k, roll(far_y[slot, :, :PLANE], k - z), pack)
        low = jnp.where((half_lane >= 6) & (half_lane < 10), corner, pack[:, :128])
        packs.append((low, pack[:, 128:]))
    first, second = packs
    for part in range(2):
        at = slice(part * 128, (part + 1) * 128)
        out_a[2, :, at] = jnp.where(odd_z, second[part], first[part])
        out_b[2, :, at] = jnp.where(odd_z, first[part], second[part])
    for slot in range(SLOTS):
        out_a[slot] = faces_z[parity_z * 2 + slot]
        out_b[slot] = faces_z[(1 - parity_z) * 2 + slot]


def pick(code, choices):
    result = choices[-1][1]
    for known, value in reversed(choices[:-1]):
        result = jnp.where(code == known, value, result)
    return result


def sign(side):
    return -1 if side == 0 else 1


def link(links, slot, dx, dy, dz):
    index = (dx + 1) * 9 + (dy + 1) * 3 + dz + 1
    value = links[slot, index if index < 13 else index - 1]
    clean = jnp.maximum(value, 0)
    return value >= 0, clean // 2, clean % 2


def whole(table, present, index):
    return jnp.where(present, table[index], jnp.zeros((CIN, PLANE), BF))


def column(table, present, index, source, side):
    target = 0 if side == 0 else EDGE - 1
    moved = pltpu.roll(table[index], (target - source + PLANE) % PLANE, 1)
    return jnp.where(present, moved, jnp.zeros((CIN, PLANE), BF))


def short(table, present, index, source, target):
    start = pl.multiple_of((source // 128) * 128, 128)
    value = table[index, :, pl.ds(start, 128)]
    moved = pltpu.roll(value, (target - source % 128 + 128) % 128, 1)
    return jnp.where(present, moved, jnp.zeros((CIN, 128), BF))


def put_corner(row, side, value):
    return jnp.where(lanes(CIN, 128) == (127 if side == 0 else EDGE), value, row)


def fill_columns(columns, buffer, centre, sides, rows):
    lane = lanes(CIN, PLANE)
    half_lane = lanes(CIN, 128)
    less = jnp.where(lane % EDGE == 0, sides[0], roll(centre, 1))
    more = jnp.where(lane % EDGE == EDGE - 1, sides[1], roll(centre, -1))
    for minor, value in enumerate((less, centre, more)):
        low, high = roll(rows[0], 1 - minor), roll(rows[1], 113 - minor)
        for major in range(3):
            start = (major * 3 + minor) * CIN
            at = slice(start, start + CIN)
            if major == 1:
                columns[buffer, at, :] = value
            elif major == 0:
                shifted = roll(value, EDGE)
                columns[buffer, at, :128] = jnp.where(half_lane < EDGE, low, shifted[:, :128])
                columns[buffer, at, 128:] = shifted[:, 128:]
            else:
                shifted = roll(value, -EDGE)
                columns[buffer, at, :128] = shifted[:, :128]
                columns[buffer, at, 128:] = jnp.where(half_lane >= 112, high, shifted[:, 128:])


def finish_second(
    links, held, wall, tie, carry, part_acc, own_a, own_b, far_a, far_b, faces_y, far_y, faces_z,
    acc, walls_z, sheets_x, sheets_y, sheets_z, columns, table
):
    parity_x, _, _ = place()
    odd_x = parity_x == 1
    for x in range(SPLIT - 1):
        at = slice(x * PLANE, (x + 1) * PLANE)
        acc[:, at] = part_acc[:, at]
    interior(
        plane_of(held), wall, columns, write_plane(acc), SPLIT, EDGE, (carry[0], carry[1])
    )
    for f in range(2):
        for tap_y in range(3):
            for tap_x in range(3):
                start = (tap_y * 3 + tap_x) * CIN
                source = (tap_y * 3 + 2 * f) * CIN
                walls_z[f, :, start : start + CIN] = wall[
                    tap_x * COUT : (tap_x + 1) * COUT, source : source + CIN
                ]
    for slot in range(SLOTS):
        a, b = own_a[slot], own_b[slot]
        table[OWN_X + slot] = jnp.where(odd_x, b, a)
        table[OWN_X + 2 + slot] = jnp.where(odd_x, a, b)
        a, b = far_a[slot], far_b[slot]
        table[FAR_X + slot] = jnp.where(odd_x, a, b)
        table[FAR_X + 2 + slot] = jnp.where(odd_x, b, a)
        table[FAR_Y + slot] = far_y[slot, :, :PLANE]
        for d in range(2):
            table[OWN_Y + d * 2 + slot] = faces_y[d * 2 + slot]
            table[EDGE_Y + d * 2 + slot, :, :128] = far_y[
                slot, :, PLANE + d * 128 : PLANE + (d + 1) * 128
            ]
            table[EDGE_Y + d * 2 + slot, :, 128:] = jnp.zeros((CIN, 128), BF)

    lane = lanes(CIN, PLANE)
    y_first, y_last = lane < EDGE, lane >= PLANE - EDGE
    zero = jnp.zeros((CIN, PLANE), BF)
    lane_o = lanes(COUT, PLANE)
    none = jnp.zeros((COUT, PLANE), F32)
    for slot in range(SLOTS):
        for d in range(2):
            present, code, u = link(links, slot, sign(d), 0, 0)
            k = d * 2 + u
            centre = whole(table, present, jnp.minimum(code, 1) * 4 + k)
            sides = []
            for f in range(2):
                present, code, u = link(links, slot, sign(d), 0, sign(f))
                index = jnp.minimum(code, 1) * 4 + d * 2 + u
                sides.append(column(table, present & (code < 4), index, last(f), f))
            rows = []
            for e in range(2):
                far = 112 if e == 0 else 0

                def index_of(code, u):
                    return pick(
                        code,
                        (
                            (0, OWN_X + d * 2 + u),
                            (1, FAR_X + d * 2 + u),
                            (2, FAR_Y + u),
                            (3, EDGE_Y + d * 2 + u),
                        ),
                    )

                def start_of(code):
                    return pick(
                        code,
                        ((0, last(e) * EDGE), (1, last(e) * EDGE), (2, last(d) * EDGE), (3, far)),
                    )

                present, code, u = link(links, slot, sign(d), sign(e), 0)
                row = short(table, present, index_of(code, u), start_of(code), 0)
                for f in range(2):
                    present, code, u = link(links, slot, sign(d), sign(e), sign(f))
                    target = 127 if f == 0 else EDGE
                    value = short(
                        table,
                        present & (code < 4),
                        index_of(code, u),
                        start_of(code) + last(f),
                        target,
                    )
                    row = put_corner(row, f, value)
                rows.append(row)
            fill_columns(columns, d, centre, sides, rows)
            taps = wall[2 * d * COUT : (2 * d + 1) * COUT, :]
            sheets_x[slot * 2 + d] = jnp.dot(taps, columns[d], preferred_element_type=F32)
        for e in range(2):
            present, code, u = link(links, slot, 0, sign(e), 0)
            centre = whole(
                table, present, jnp.where(code == 0, OWN_Y + e * 2 + u, FAR_Y + u)
            )
            sides = []
            for f in range(2):
                present, code, u = link(links, slot, 0, sign(e), sign(f))
                index = jnp.where(code == 0, OWN_Y + e * 2 + u, FAR_Y + u)
                sides.append(column(table, present & (code < 4), index, last(f), f))
            columns[e, :CIN, :] = jnp.where(lane % EDGE == 0, sides[0], roll(centre, 1))
            columns[e, CIN : 2 * CIN, :] = centre
            columns[e, 2 * CIN : 3 * CIN, :] = jnp.where(
                lane % EDGE == EDGE - 1, sides[1], roll(centre, -1)
            )
            taps = wall[:, 2 * e * 3 * CIN : (2 * e + 1) * 3 * CIN]
            part = jnp.dot(taps, columns[e, : 3 * CIN, :], preferred_element_type=F32)
            sheet = part[COUT : 2 * COUT]
            sheet = sheet + jnp.where(lane_o < EDGE, none, roll(part[:COUT], EDGE))
            sheet = sheet + jnp.where(
                lane_o >= PLANE - EDGE, none, roll(part[2 * COUT :], -EDGE)
            )
            sheets_y[slot * 2 + e] = sheet
        for f in range(2):
            present, code, u = link(links, slot, 0, 0, sign(f))
            centre = jnp.where(present & (code < 4), faces_z[f * 2 + u], zero)
            columns[f, :CIN, :] = jnp.where(y_first, zero, roll(centre, EDGE))
            columns[f, CIN : 2 * CIN, :] = centre
            columns[f, 2 * CIN : 3 * CIN, :] = jnp.where(y_last, zero, roll(centre, -EDGE))
            taps = jnp.concatenate(
                [
                    wall[:, (tap_y * 3 + 2 * f) * CIN : (tap_y * 3 + 2 * f + 1) * CIN]
                    for tap_y in range(3)
                ],
                1,
            )
            part = jnp.dot(taps, columns[f, : 3 * CIN, :], preferred_element_type=F32)
            sheet = part[COUT : 2 * COUT]
            sheet = sheet + jnp.where(lane_o % EDGE == 0, none, roll(part[:COUT], 1))
            sheet = sheet + jnp.where(
                lane_o % EDGE == EDGE - 1, none, roll(part[2 * COUT :], -1)
            )
            sheets_z[slot * 2 + f] = sheet


def finish(
    links, count, acc_a, acc_b, sheets_x, sheets_y, near_z, got_a, got_b, walls_z, bias, head,
    head_bias, turn, out, columns, table
):
    _, parity_z, _ = place()
    odd_z = parity_z == 1
    for slot in range(SLOTS):
        a, b = got_a[slot], got_b[slot]
        table[FAR_Z + slot] = jnp.where(odd_z, a, b)
        table[FAR_Z + 2 + slot] = jnp.where(odd_z, b, a)
    a, b = got_a[2], got_b[2]
    for f, value in enumerate((jnp.where(odd_z, a, b), jnp.where(odd_z, b, a))):
        table[EDGE_Z + f] = value
        table[TURN_Z + f] = jnp.dot(value, turn[...], preferred_element_type=F32).astype(BF)
    accs = (acc_a, acc_b)
    lane_o = lanes(COUT, PLANE)
    half_o = lanes(COUT, 128)
    none = jnp.zeros((COUT, PLANE), F32)
    half_none = jnp.zeros((COUT, 128), F32)
    for slot in range(SLOTS):
        acc = accs[slot]
        sheets_z = []
        for f in range(2):
            present, code, u = link(links, slot, 0, 0, sign(f))
            centre = whole(table, present & (code >= 4), FAR_Z + f * 2 + u)
            sides = []
            for d in range(2):
                present, code, u = link(links, slot, sign(d), 0, sign(f))
                index = jnp.where(code == 4, FAR_Z + f * 2 + u, EDGE_Z + f)
                source = jnp.where(code == 4, last(d), d * 2 + u)
                sides.append(column(table, present & (code >= 4), index, source, d))
            rows = []
            for e in range(2):
                present, code, u = link(links, slot, 0, sign(e), sign(f))
                index = jnp.where(code == 4, FAR_Z + f * 2 + u, TURN_Z + f)
                source = jnp.where(code == 4, last(e) * EDGE, (4 + u) * EDGE)
                row = short(table, present & (code >= 4), index, source, 0)
                for d in range(2):
                    present, code, u = link(links, slot, sign(d), sign(e), sign(f))
                    index = jnp.where(code == 4, FAR_Z + f * 2 + u, EDGE_Z + f)
                    source = pick(
                        code,
                        (
                            (4, last(e) * EDGE + last(d)),
                            (5, last(e) * EDGE + d * 2 + u),
                            (6, last(d) * EDGE + 4 + u),
                            (7, 6 + d * 2 + u),
                        ),
                    )
                    target = 127 if d == 0 else EDGE
                    value = short(table, present & (code >= 4), index, source, target)
                    row = put_corner(row, d, value)
                rows.append(row)
            fill_columns(columns, f, centre, sides, rows)
            sheets_z.append(
                near_z[slot * 2 + f]
                + jnp.dot(walls_z[f], columns[f], preferred_element_type=F32)
            )
        used = slot < count[0]
        for x in range(EDGE):
            total = acc[:, x * PLANE : (x + 1) * PLANE]
            if x == 0:
                total = total + sheets_x[slot * 2]
            elif x == EDGE - 1:
                total = total + sheets_x[slot * 2 + 1]
            total = total + jnp.where(lane_o % EDGE == 0, roll(sheets_z[0], -x), none)
            total = total + jnp.where(
                lane_o % EDGE == EDGE - 1, roll(sheets_z[1], EDGE - 1 - x), none
            )
            from_half = slice((x // 8) * 128, (x // 8 + 1) * 128)
            low = roll(sheets_y[slot * 2, :, from_half], -(x % 8) * EDGE)
            high = roll(sheets_y[slot * 2 + 1, :, from_half], 112 - (x % 8) * EDGE)
            low = total[:, :128] + jnp.where(half_o < EDGE, low, half_none)
            high = total[:, 128:] + jnp.where(half_o >= 112, high, half_none)
            for part, value in enumerate((low, high)):
                hidden = jnp.maximum(value + bias[...], 0.0).astype(BF)
                mixed = jnp.dot(head[...], hidden, preferred_element_type=F32) + head_bias[...]
                out[slot, :, x * PLANE + part * 128 : x * PLANE + (part + 1) * 128] = jnp.where(
                    used, mixed, half_none
                ).astype(BF)


SMEM = pl.BlockSpec(memory_space=pltpu.SMEM)
VMEM = pl.BlockSpec(memory_space=pltpu.VMEM)
HBM = pl.BlockSpec(memory_space=pltpu.HBM)
ANY = pl.BlockSpec(memory_space=pl.ANY)


def shape(dims, kind=BF):
    return jax.ShapeDtypeStruct(dims, kind)


def in_hbm(value):
    return pltpu.with_memory_space_constraint(value, pltpu.HBM)


def swap(first, second, axis):
    length = lax.axis_size(axis)
    even = [(i, i ^ 1) for i in range(length)]
    odd = [(i, ((i + 1) ^ 1) - 1) for i in range(1, length - 1)]
    return lax.ppermute(first, axis, even), lax.ppermute(second, axis, odd)


def body(blocks, block_count, neighbours, conv_weight, conv_bias, head_weight, head_bias):
    volumes = blocks.reshape(SLOTS, CIN, VOX)
    count = block_count.reshape(1)
    links = neighbours.reshape(SLOTS, 26)
    odd_x = lax.axis_index("gx") % 2
    far_end = VOX - PLANE
    own_a = lax.dynamic_slice_in_dim(volumes, (1 - odd_x) * far_end, PLANE, 2)
    own_b = lax.dynamic_slice_in_dim(volumes, odd_x * far_end, PLANE, 2)
    far_a, far_b = swap(own_a, own_b, "gx")
    buffer = pltpu.VMEM((2, TAPS * CIN, PLANE), BF)
    block_flops = 2 * COUT * 27 * CIN * VOX
    held, faces_y, faces_z, acc_a, wall = pl.pallas_call(
        pack_and_convolve,
        out_shape=(
            shape((CIN, VOX)),
            shape((4, CIN, PLANE)),
            shape((4, CIN, PLANE)),
            shape((COUT, VOX), F32),
            shape((3 * COUT, TAPS * CIN)),
        ),
        in_specs=[HBM, HBM],
        out_specs=(VMEM, VMEM, VMEM, VMEM, VMEM),
        scratch_shapes=[
            buffer,
            pltpu.VMEM((CIN, VOX), BF),
            pltpu.VMEM((COUT, 27 * CIN), BF),
            pltpu.SemaphoreType.DMA((SLOTS * CHUNK,)),
            pltpu.SemaphoreType.DMA,
        ],
        compiler_params=params(16),
        cost_estimate=pl.CostEstimate(
            flops=2 * block_flops, bytes_accessed=4 * 2**20, transcendentals=0
        ),
    )(in_hbm(volumes), in_hbm(conv_weight))
    sent_y = pl.pallas_call(
        pack_for_y,
        out_shape=shape((SLOTS, CIN, 2 * PLANE)),
        in_specs=[VMEM, VMEM, VMEM],
        out_specs=VMEM,
        compiler_params=params(8),
    )(faces_y, far_a, far_b)
    far_y = lax.ppermute(sent_y, "gy", [(0, 1), (1, 0)])
    part_acc, carry = pl.pallas_call(
        begin_second,
        out_shape=(shape((COUT, (SPLIT - 1) * PLANE), F32), shape((2, COUT, PLANE), F32)),
        in_specs=[VMEM, VMEM, ANY],
        out_specs=(VMEM, VMEM),
        scratch_shapes=[buffer],
        compiler_params=params(16),
        cost_estimate=pl.CostEstimate(
            flops=block_flops, bytes_accessed=2**20, transcendentals=0
        ),
    )(held, wall, sent_y)
    sent_a, sent_b = pl.pallas_call(
        pack_for_z,
        out_shape=(shape((3, CIN, PLANE)), shape((3, CIN, PLANE))),
        in_specs=[VMEM, VMEM, VMEM, VMEM],
        out_specs=(VMEM, VMEM),
        compiler_params=params(8),
    )(faces_z, far_a, far_b, far_y)
    got_a, got_b = swap(sent_a, sent_b, "gz")
    sheet = shape((4, COUT, PLANE), F32)
    acc_b, walls_z, sheets_x, sheets_y, near_z = pl.pallas_call(
        finish_second,
        out_shape=(
            shape((COUT, VOX), F32), shape((2, COUT, TAPS * CIN)), sheet, sheet, sheet
        ),
        in_specs=[SMEM, VMEM, VMEM, ANY] + [VMEM] * 9,
        out_specs=(VMEM,) * 5,
        scratch_shapes=[buffer, pltpu.VMEM((NEAR_SOURCES, CIN, PLANE), BF)],
        compiler_params=params(16),
        cost_estimate=pl.CostEstimate(
            flops=2 * block_flops, bytes_accessed=2 * 2**20, transcendentals=0
        ),
    )(
        links, held, wall, sent_a, carry, part_acc, own_a, own_b, far_a, far_b, faces_y, far_y,
        faces_z,
    )
    index = jnp.arange(PLANE)
    turn = (index[:, None] == (index % EDGE * EDGE + index // EDGE)[None, :]).astype(BF)
    outputs = pl.pallas_call(
        finish,
        out_shape=shape((SLOTS, COUT, VOX)),
        in_specs=[SMEM] * 2 + [VMEM] * 12,
        out_specs=VMEM,
        scratch_shapes=[buffer, pltpu.VMEM((Z_SOURCES, CIN, PLANE), BF)],
        compiler_params=params(16),
    )(
        links, count, acc_a, acc_b, sheets_x, sheets_y, near_z, got_a, got_b, walls_z,
        conv_bias.reshape(COUT, 1), head_weight, head_bias.reshape(COUT, 1), turn,
    )
    return outputs.reshape(1, 1, SLOTS, COUT, VOX)


def solution(mesh):
    placed = (
        P("gx", "gz", "gy", None, None),
        P("gx", "gz", "gy"),
        P("gx", "gz", "gy", None),
        P(),
        P(),
        P(),
        P(),
    )
    return jax.shard_map(
        body, mesh=mesh, in_specs=placed, out_specs=P("gx", "gz", "gy", None, None), check_vma=False
    )
```

time: 35.1 us -> 31.2 us (0.89)
  the two profiles are of different devices: /device:TPU:78 before, /device:TPU:103 now
where the time goes in v2:
time: 31.2 us; the launch traced here: 31.1 us
  Pallas kernels  16.5 us (53%)
  starting transfers between devices  12.5 us (40%)
  local copies, waits for them, and re-layouts  1.16 us (4%)
  between operations  0.83 us (3%)
    ppermute x4, starting transfers between devices, swap(): return (lax.ppermute(first, axis, even), lax.ppermute(second, axis, odd))  11.2 us
    pallas_call x1, Pallas kernels, body(): pl.pallas_call(pack_and_convolve, out_shape=(shape((CIN, VOX)), shape((4,...  5.24 us
    pallas_call x1, Pallas kernels, body(): pl.pallas_call(finish, out_shape=shape((SLOTS, COUT, VOX)), in_specs=[SME...  5.21 us
    pallas_call x1, Pallas kernels, body(): pl.pallas_call(finish_second, out_shape=(shape((COUT, VOX), F32), shape((...  4.77 us
    ppermute x1, starting transfers between devices, body(): far_y = lax.ppermute(sent_y, 'gy', [(0, 1), (1, 0)])  1.33 us
    dynamic_slice x1, local copies, waits for them, and re-layouts, body(): own_b = lax.dynamic_slice_in_dim(volumes, odd_x * far_end, PLANE, 2)  0.95 us
    pallas_call x1, Pallas kernels, body(): pl.pallas_call(begin_second, out_shape=(shape((COUT, (SPLIT - 1) * PLANE)...  0.95 us
  transfers between devices with their start and end apart: 5, of which 0 were waited for; matrix products, arithmetic and copies ran while one was open for 1% of the time, Pallas kernels for 35%

profile of v2, /device:TPU:103, one launch (start us, length us, event | category | flops | bytes accessed | tf_op | source)
XLA Modules:
  0.0 31.1 jit_solution(2532461386518716472)
XLA Ops:
  0.0 1.0 %dynamic-slice_bitcast_fusion = (bf16[2,96,256]{2,1,0:T(8,128)(2,1)S(1)}, bf16[2,96,256]{2,1,0:T(8,128)(2,1)S(1)}) fusion(bf16[1,1,2,96,4096]{4,3,2,1,0:T(8,128)(2,1)} %param.7, s32[]{:T(128)S(6)} %select_n.34, s32[]{:T(128)S(6)} %select_n.33), kind=kLoop, calls=%fused_computation.2 | loop fusion | bytes 393224 | tf_op jit(solution)/shard_map/dynamic_slice | solution.py:497
  1.0 1.4 %collective-permute-start = (bf16[2,96,256]{2,1,0:T(8,128)(2,1)S(1)}, bf16[2,96,256]{2,1,0:T(8,128)(2,1)S(1)}, u32[]{:S(2)}, u32[]{:S(2)}) collective-permute-start(bf16[2,96,256]{2,1,0:T(8,128)(2,1)S(1)} %get-tuple-element.34.own_a), channel_id=1, source_target_pairs={{0,16},{16,0},{32,48},{48,32},{64,80},{80,64},{96,112},{112,96},{1... | collective-permute-start | bytes 294920 | tf_op jit(solution)/shard_map/ppermute | solution.py:487
  2.3 4.1 %collective-permute-start.1 = (bf16[2,96,256]{2,1,0:T(8,128)(2,1)S(1)}, bf16[2,96,256]{2,1,0:T(8,128)(2,1)S(1)}, u32[]{:S(2)}, u32[]{:S(2)}) collective-permute-start(bf16[2,96,256]{2,1,0:T(8,128)(2,1)S(1)} %get-tuple-element.33.own_b), channel_id=1, source_target_pairs={{16,32},{32,16},{48,64},{64,48},{80,96},{96,80},{112,128},{128,112... | collective-permute-start | bytes 294920 | tf_op jit(solution)/shard_map/ppermute | solution.py:487
  6.4 0.0 copy-start.2
  6.4 0.0 copy-start.3
  6.4 5.2 %shard_map.73 = (bf16[96,4096]{1,0:T(8,128)(2,1)S(1)}, bf16[4,96,256]{2,1,0:T(8,128)(2,1)S(1)}, bf16[4,96,256]{2,1,0:T(8,128)(2,1)S(1)}, f32[48,4096]{1,0:T(8,128)S(1)}, bf16[144,864]{1,0:T(8,128)(2,1)S(1)}) custom-call(bf16[2,96,4096]{2,1,0:T(8,128)(2,1)} %bitcast.13, bf16[48,2592]{1,0:T(8,128)(2,1)} %weight.1), custom_call_target="tpu_custom_call" | custom-call | flops 2038431744 | bytes 4194304 | tf_op jit(solution)/shard_map/pallas_call | solution.py:501
  11.7 0.0 collective-permute-done.far_a
  11.7 0.0 collective-permute-done.1.far_b
  11.8 1.3 %collective-permute-start.2 = (bf16[2,96,512]{2,1,0:T(8,128)(2,1)S(1)}, bf16[2,96,512]{2,1,0:T(8,128)(2,1)S(1)}, u32[]{:S(2)}, u32[]{:S(2)}) collective-permute-start(bf16[2,96,512]{2,1,0:T(8,128)(2,1)S(1)} %shard_map.74.tie), channel_id=1, source_target_pairs={{0,1},{1,0},{2,3},{3,2},{4,5},{5,4},{6,7},{7,6},{8,9},{9,8},{10,11... | collective-permute-start | bytes 589832 | tf_op jit(solution)/shard_map/ppermute | solution.py:531
  13.1 0.0 copy-done.2
  13.1 0.1 copy.8.bias
  13.2 0.0 copy-done.3
  13.2 0.1 copy.9.head_bias
  14.0 0.0 copy-start.1
  14.0 1.0 %shard_map.76 = (f32[48,1024]{1,0:T(8,128)S(1)}, f32[2,48,256]{2,1,0:T(8,128)S(1)}) custom-call(bf16[96,4096]{1,0:T(8,128)(2,1)S(1)} %get-tuple-element.20.held, bf16[144,864]{1,0:T(8,128)(2,1)S(1)} %get-tuple-element.21.wall, bf16[2,96,512]{2,1,0:T(8,128)(2,1)S(1)} %shard_map.74.tie), custom_call_target="tpu_custom_call" | custom-call | flops 1019215872 | bytes 1048576 | tf_op jit(solution)/shard_map/pallas_call | solution.py:532
  15.0 0.0 collective-permute-done.2.far_y
  15.0 0.3 shard_map.75
  15.3 0.1 collective-permute-start.3
  15.4 5.6 %collective-permute-start.4 = (bf16[3,96,256]{2,1,0:T(8,128)(2,1)S(1)}, bf16[3,96,256]{2,1,0:T(8,128)(2,1)S(1)}, u32[]{:S(2)}, u32[]{:S(2)}) collective-permute-start(bf16[3,96,256]{2,1,0:T(8,128)(2,1)S(1)} %get-tuple-element.31), channel_id=1, source_target_pairs={{2,4},{4,2},{6,8},{8,6},{10,12},{12,10},{3,5},{5,3},{7,9},{9,7},{1... | collective-permute-start | bytes 442376 | tf_op jit(solution)/shard_map/ppermute | solution.py:487
  21.0 0.0 copy-done.1
  21.0 0.0 copy-start
  21.0 4.8 %shard_map.77 = (f32[48,4096]{1,0:T(8,128)S(1)}, bf16[2,48,864]{2,1,0:T(8,128)(2,1)S(1)}, f32[4,48,256]{2,1,0:T(8,128)S(1)}, f32[4,48,256]{2,1,0:T(8,128)S(1)}, f32[4,48,256]{2,1,0:T(8,128)S(1)}) custom-call(s32[2,26]{1,0:T(2,128)S(1)} %bitcast.11, bf16[96,4096]{1,0:T(8,128)(2,1)S(1)} %get-tuple-element.20.held, ...), custom_call_target="tpu_custom_call" | custom-call | flops 2038431744 | bytes 2097152 | tf_op jit(solution)/shard_map/pallas_call | solution.py:552
  25.8 0.0 collective-permute-done.3.got_a
  25.8 0.0 collective-permute-done.4.got_b
  25.8 0.0 copy-done
  25.8 5.2 %shard_map.78 = bf16[2,48,4096]{2,1,0:T(8,128)(2,1)} custom-call(s32[2,26]{1,0:T(2,128)S(1)} %bitcast.12, s32[1]{0:T(128)} %bitcast.10.count, f32[48,4096]{1,0:T(8,128)S(1)} %get-tuple-element.19.acc_a, f32[48,4096]{1,0:T(8,128)S(1)} %get-tuple-element.27.acc_b, f32[4,48,256]{2,1,0:T(8,128)S(1)} %get-tuple-element.28.sheets_x, ...), custom_call_target="tpu_custom_call" | custom-call | tf_op jit(solution)/shard_map/pallas_call | solution.py:570
  (3 shorter events, 0.1 us)
Async XLA Ops:
  1.0 10.7 %collective-permute-start = (bf16[2,96,256]{2,1,0:T(8,128)(2,1)S(1)}, bf16[2,96,256]{2,1,0:T(8,128)(2,1)S(1)}, u32[]{:S(2)}, u32[]{:S(2)}) collective-permute-start(bf16[2,96,256]{2,1,0:T(8,128)(2,1)S(1)} %get-tuple-element.34.own_a), channel_id=1, source_target_pairs={{0,16},{16,0},{32,48},{48,32},{64,80},{80,64},{96,112},{112,96},{1... | collective-permute-start | bytes 294920 | tf_op jit(solution)/shard_map/ppermute | solution.py:487
  2.3 9.4 %collective-permute-start.1 = (bf16[2,96,256]{2,1,0:T(8,128)(2,1)S(1)}, bf16[2,96,256]{2,1,0:T(8,128)(2,1)S(1)}, u32[]{:S(2)}, u32[]{:S(2)}) collective-permute-start(bf16[2,96,256]{2,1,0:T(8,128)(2,1)S(1)} %get-tuple-element.33.own_b), channel_id=1, source_target_pairs={{16,32},{32,16},{48,64},{64,48},{80,96},{96,80},{112,128},{128,112... | collective-permute-start | bytes 294920 | tf_op jit(solution)/shard_map/ppermute | solution.py:487
  6.4 6.7 %copy-start.2 = (f32[48]{0:T(128)S(1)}, f32[48]{0:T(128)}, u32[]{:S(2)}) copy-start(f32[48]{0:T(128)} %param.11) | copy-start | bytes 580
  6.4 6.8 %copy-start.3 = (f32[48]{0:T(128)S(1)}, f32[48]{0:T(128)}, u32[]{:S(2)}) copy-start(f32[48]{0:T(128)} %param.13) | copy-start | bytes 580
  11.8 3.2 %collective-permute-start.2 = (bf16[2,96,512]{2,1,0:T(8,128)(2,1)S(1)}, bf16[2,96,512]{2,1,0:T(8,128)(2,1)S(1)}, u32[]{:S(2)}, u32[]{:S(2)}) collective-permute-start(bf16[2,96,512]{2,1,0:T(8,128)(2,1)S(1)} %shard_map.74.tie), channel_id=1, source_target_pairs={{0,1},{1,0},{2,3},{3,2},{4,5},{5,4},{6,7},{7,6},{8,9},{9,8},{10,11... | collective-permute-start | bytes 589832 | tf_op jit(solution)/shard_map/ppermute | solution.py:531
  14.0 7.0 %copy-start.1 = (s32[1,1,2,26]{3,2,1,0:T(2,128)S(1)}, s32[1,1,2,26]{3,2,1,0:T(2,128)}, u32[]{:S(2)}) copy-start(s32[1,1,2,26]{3,2,1,0:T(2,128)} %param.9) | copy-start | bytes 628
  15.3 10.6 %collective-permute-start.3 = (bf16[3,96,256]{2,1,0:T(8,128)(2,1)S(1)}, bf16[3,96,256]{2,1,0:T(8,128)(2,1)S(1)}, u32[]{:S(2)}, u32[]{:S(2)}) collective-permute-start(bf16[3,96,256]{2,1,0:T(8,128)(2,1)S(1)} %get-tuple-element.24.tie), channel_id=1, source_target_pairs={{0,2},{2,0},{4,6},{6,4},{8,10},{10,8},{12,14},{14,12},{1,3},{3,1},... | collective-permute-start | bytes 442376 | tf_op jit(solution)/shard_map/ppermute | solution.py:487
  15.4 10.5 %collective-permute-start.4 = (bf16[3,96,256]{2,1,0:T(8,128)(2,1)S(1)}, bf16[3,96,256]{2,1,0:T(8,128)(2,1)S(1)}, u32[]{:S(2)}, u32[]{:S(2)}) collective-permute-start(bf16[3,96,256]{2,1,0:T(8,128)(2,1)S(1)} %get-tuple-element.31), channel_id=1, source_target_pairs={{2,4},{4,2},{6,8},{8,6},{10,12},{12,10},{3,5},{5,3},{7,9},{9,7},{1... | collective-permute-start | bytes 442376 | tf_op jit(solution)/shard_map/ppermute | solution.py:487
  21.0 4.8 %copy-start = (bf16[48,48]{1,0:T(8,128)(2,1)S(1)}, bf16[48,48]{1,0:T(8,128)(2,1)}, u32[]{:S(2)}) copy-start(bf16[48,48]{1,0:T(8,128)(2,1)} %head.1) | copy-start | bytes 13828
